TPU v7x, 256 devices: a whole 4x4x8 slice. The times are simulated.
256 devices in a mesh: fsdp: 8 (over x, core), tp: 32 (over y, z).
Axes of the slice: x: 4, y: 4, z: 8, core: 2. Of those that a mesh axis runs over, the one named last changes fastest.
Arguments:
- momentum: float32 [8192, 28672], P('fsdp', 'tp'), may hold values from -6 to 6
- gradient: bfloat16 [8192, 28672], P('fsdp', 'tp'), may hold values from -6 to 6
- right_factor: float32 [512, 28672], P('fsdp', 'tp'), may hold values from -0.03125 to 0.03125
Outputs:
- new_momentum: float32 [8192, 28672], P('fsdp', 'tp')
- update: bfloat16 [8192, 28672], P('fsdp', 'tp')
- new_factor: float32 [512, 28672], P('fsdp', 'tp')
All inputs are finite; a program needn't handle non-finite values.
Results may differ from a plain program's by a relative error of at most 0.001.
Values sent between devices are 32-bit elements; how exact they have to be, the bound alone decides.
No kernel may reach another device: no remote copies, remote signals or barrier semaphores. Data moves between devices by JAX's collectives and lax.ppermute only.
A program may use at most 64 MiB of HBM per device.

v0:
```python
import math

import jax
import jax.numpy as jnp
from jax import lax
from jax.sharding import PartitionSpec as P

D = 8192
FF = 28672
RANK = 512


decay_rest = 0.05
epsilon = 1e-06


def product(left, right):
    return jnp.dot(left, right, precision=lax.Precision.HIGHEST, preferred_element_type=jnp.float32)


def against(rows, factor):
    return lax.dot_general(
        rows,
        factor,
        (((1,), (1,)), ((), ())),
        precision=lax.Precision.HIGHEST,
        preferred_element_type=jnp.float32,
    )


def orthonormal(gram, left):
    lower = jnp.linalg.cholesky(gram)
    return jax.scipy.linalg.solve_triangular(lower, left.T, lower=True).T


def per_device(momentum, gradient, right_factor):
    combined = momentum + gradient.astype(jnp.float32)
    whole_factor = lax.all_gather(right_factor, "fsdp", axis=0, tiled=True)
    left = lax.psum(against(combined, whole_factor), "tp")
    gram = lax.psum(product(left.T, left), "fsdp")
    orth = orthonormal(gram, left)
    block = right_factor.shape[0]
    right = lax.psum(product(orth.T, combined), "fsdp")
    squared = lax.psum(jnp.sum(right * right, axis=1), "tp")
    norms = jnp.sqrt(squared + epsilon)
    factor_full = right / norms[:, None]
    new_factor = lax.dynamic_slice_in_dim(factor_full, lax.axis_index("fsdp") * block, block, 0)
    new_momentum = combined - decay_rest * product(orth, right)
    scale_rms = math.sqrt(D * FF / RANK)
    update = (scale_rms * product(orth, factor_full)).astype(jnp.bfloat16)
    return (new_momentum, update, new_factor)


def solution(mesh):
    in_specs = (P("fsdp", "tp"), P("fsdp", "tp"), P("fsdp", "tp"))
    out_specs = (P("fsdp", "tp"), P("fsdp", "tp"), P("fsdp", "tp"))
    return jax.shard_map(
        per_device, mesh=mesh, in_specs=in_specs, out_specs=out_specs, check_vma=False
    )
```

profile of v0, /device:TPU:0, one launch (start us, length us, event | category | flops | bytes accessed | tf_op | source)
XLA Modules:
  0.0 612.3 jit_solution(6653306843217127422)
XLA Ops:
  7.2 0.7 all-gather.2.cloned.1.call-update
  7.9 30.6 %all-gather.2.cloned.1.call-done = f32[512,896]{1,0:T(8,128)} async-done(((f32[64,896]{1,0:T(8,128)}), f32[512,896]{1,0:T(8,128)}) %all-gather.2.cloned.1.call-update) | async-done | bytes 1835024 | tf_op jit(solution)/shard_map/all_gather | solution.py:38
  38.6 10.3 %fusion.7 = f32[1024,512]{1,0:T(8,128)} fusion(f32[512,896]{1,0:T(8,128)} %all-gather.2.cloned.1.call-done, f32[1024,896]{1,0:T(8,128)} %param.3, bf16[1024,896]{1,0:T(8,128)(2,1)} %param.4), kind=kOutput, calls=%fused_computation.14 | convolution fusion | flops 5638979584 | bytes 9437184 | tf_op jit(solution)/shard_map/dot_general | solution.py:22
  49.0 154.6 %all-reduce.5.cloned.1.call-done = f32[1024,512]{1,0:T(8,128)} async-done(((f32[1024,512]{1,0:T(8,128)}), f32[1024,512]{1,0:T(8,128)}) %all-reduce.5.cloned.1.call-update) | async-done | bytes 2097168 | tf_op jit(solution)/shard_map/psum | solution.py:39
  203.5 6.7 %fusion.40 = f32[512,512]{0,1:T(8,128)} fusion(f32[1024,512]{1,0:T(8,128)} %all-reduce.5.cloned.1.call-done), kind=kOutput, calls=%fused_computation.80 | convolution fusion | flops 3221225472 | bytes 3145728 | tf_op jit(solution)/shard_map/dot_general | solution.py:18
  210.5 64.2 %all-reduce.7.cloned.1.call-done = f32[512,512]{0,1:T(8,128)} async-done(((f32[512,512]{0,1:T(8,128)}), f32[512,512]{0,1:T(8,128)}) %all-reduce.7.cloned.1.call-update) | async-done | bytes 1048592 | tf_op jit(solution)/shard_map/psum | solution.py:40
  274.7 1.6 copy.7
  276.6 1.0 copy-done.11
  277.6 11.7 %cholesky.104 = f32[128,128]{1,0:T(8,128)S(1)} custom-call(f32[128,128]{1,0:T(8,128)S(1)} %cholesky.266), custom_call_target="Cholesky" | custom-call | tf_op jit(solution)/shard_map/jit(cholesky)/cholesky | solution.py:32
  289.5 9.8 %custom-call.31 = f32[1,128,128]{1,2,0:T(8,128)S(1)} custom-call(f32[1,128,128]{2,1,0:T(8,128)S(1)} %get-tuple-element.30), custom_call_target="InvertDiagBlocksLowerTriangular" | custom-call | tf_op jit(solution)/shard_map/jit(cholesky)/cholesky | solution.py:32
  299.3 1.2 constant_dynamic-update-slice_fusion.3
  300.6 1.3 convolution_subtract_fusion.2
  301.8 11.7 %cholesky.217 = f32[128,128]{1,0:T(8,128)S(1)} custom-call(f32[128,128]{1,0:T(8,128)S(1)} %cholesky.270), custom_call_target="Cholesky" | custom-call | tf_op jit(solution)/shard_map/jit(cholesky)/cholesky | solution.py:32
  313.6 10.2 %custom-call.32 = f32[1,128,128]{1,2,0:T(8,128)S(1)} custom-call(f32[1,128,128]{2,1,0:T(8,128)S(1)} %get-tuple-element.27), custom_call_target="InvertDiagBlocksLowerTriangular" | custom-call | tf_op jit(solution)/shard_map/jit(cholesky)/cholesky | solution.py:32
  324.0 1.3 convolution_subtract_fusion.3
  325.4 11.7 %cholesky.238 = f32[128,128]{1,0:T(8,128)S(1)} custom-call(f32[128,128]{1,0:T(8,128)S(1)} %cholesky.275), custom_call_target="Cholesky" | custom-call | tf_op jit(solution)/shard_map/jit(cholesky)/cholesky | solution.py:32
  337.1 9.8 %custom-call.33 = f32[1,128,128]{1,2,0:T(8,128)S(1)} custom-call(f32[1,128,128]{2,1,0:T(8,128)S(1)} %get-tuple-element.24), custom_call_target="InvertDiagBlocksLowerTriangular" | custom-call | tf_op jit(solution)/shard_map/jit(cholesky)/cholesky | solution.py:32
  347.1 1.2 convolution_subtract_fusion.4
  348.4 11.7 %cholesky.255 = f32[128,128]{1,0:T(8,128)S(1)} custom-call(f32[128,128]{1,0:T(8,128)S(1)} %convolution_subtract_fusion.4), custom_call_target="Cholesky" | custom-call | tf_op jit(solution)/shard_map/jit(cholesky)/cholesky | solution.py:32
  360.1 0.6 compare_reduce_fusion.1
  360.8 0.7 compare_reduce_fusion
  361.4 0.6 compare_reduce_fusion.2
  364.6 1.3 select_select_fusion
  365.8 13.8 %while.1 = (s32[]{:T(128)}, f32[512,512]{1,0:T(8,128)}, s32[4,2]{0,1:T(2,128)S(1)}, f32[4,128,128]{2,1,0:T(8,128)}, s32[]{:T(128)}) while((s32[]{:T(128)}, f32[512,512]{1,0:T(8,128)}, s32[4,2]{0,1:T(2,128)S(1)}, f32[4,128,128]{2,1,0:T(8,128)}, s32[]{:T(128)}) %tuple.31), condition=%wide.while_cond, body=%wide.while_body.sunk | while | flops 2 | bytes 132205 | solution.py:33
  365.9 0.5 fusion.52
  366.4 2.9 bitcast_dynamic-update-slice_fusion.2
  369.4 0.5 fusion.52
  369.9 2.9 bitcast_dynamic-update-slice_fusion.2
  372.9 0.5 fusion.52
  373.4 2.9 bitcast_dynamic-update-slice_fusion.2
  376.9 2.8 bitcast_dynamic-update-slice_fusion.2
  379.7 40.1 %custom-call.34 = f32[4,128,128]{1,2,0:T(8,128)S(1)} custom-call(f32[4,128,128]{2,1,0:T(8,128)} %get-tuple-element.10), custom_call_target="InvertDiagBlocksLowerTriangular" | custom-call | tf_op jit(solution)/shard_map/jit(_solve_triangular)/triangular_solve | solution.py:33
  419.8 0.6 fusion.15
  420.5 1.8 convolution_subtract_fusion.1
  422.3 0.6 fusion.28
  423.0 2.8 convolution_subtract_fusion
  425.8 0.6 fusion.26
  426.5 3.9 fusion.8
  430.4 0.6 fusion.25
  431.0 0.8 copy-done.8
  431.8 8.4 %fusion.6 = f32[512,896]{1,0:T(8,128)} fusion(f32[1024,896]{1,0:T(8,128)S(1)} %copy-done, bf16[1024,896]{1,0:T(8,128)(2,1)S(1)} %copy-done.3, f32[128,1024]{1,0:T(8,128)S(1)} %fusion.25, f32[128,1024]{1,0:T(8,128)S(1)} %fusion.26, f32[128,1024]{1,0:T(8,128)S(1)} %fusion.28, f32[128,1024]{1,0:T(8,128)S(1)} %fusion.15), kind=kOutput, calls=%fused_computation.13 | convolution fusion | flops 5640552448 | bytes 9437184 | tf_op jit(solution)/shard_map/dot_general | solution.py:18
  440.2 69.4 %all-reduce.9.cloned.1.call-done = f32[512,896]{1,0:T(8,128)} async-done(((f32[512,896]{1,0:T(8,128)}), f32[512,896]{1,0:T(8,128)}) %all-reduce.9.cloned.1.call-update) | async-done | bytes 1835024 | tf_op jit(solution)/shard_map/psum | solution.py:43
  509.7 1.8 multiply_reduce_fusion
  511.5 75.1 %psum.31 = f32[512]{0:T(512)S(1)} all-reduce(f32[512]{0:T(512)S(1)} %multiply_reduce_fusion), channel_id=1, replica_groups=mesh['fsdp'=8,'tp'=32] {'tp'}, use_global_device_ids=true, to_apply=%region_12.13 | all-reduce | flops 512 | bytes 4096 | tf_op jit(solution)/shard_map/psum | solution.py:44
  586.8 0.8 copy-done.7
  587.8 8.0 %multiply_convert_fusion = bf16[1024,896]{1,0:T(8,128)(2,1)} fusion(f32[512,896]{1,0:T(8,128)S(1)} %broadcast_divide_fusion, f32[128,1024]{1,0:T(8,128)S(1)} %copy-done.9, f32[128,1024]{1,0:T(8,128)S(1)} %copy-done.7, f32[128,1024]{1,0:T(8,128)S(1)} %fusion.28, f32[128,1024]{1,0:T(8,128)S(1)} %fusion.15), kind=kOutput, calls=%fused_computation.2 | convolution fusion | flops 5640552448 | bytes 5767168 | tf_op jit(solution)/shard_map/dot_general | solution.py:18
  595.8 0.7 constant_dynamic-slice_fusion.1
  596.5 9.0 %multiply_subtract_fusion = f32[1024,896]{1,0:T(8,128)} fusion(f32[512,896]{1,0:T(8,128)S(1)} %copy-done.5, f32[1024,896]{1,0:T(8,128)S(1)} %copy-done.1, bf16[1024,896]{1,0:T(8,128)(2,1)S(1)} %copy-done.4, f32[128,1024]{1,0:T(8,128)S(1)} %copy-done.9, f32[128,1024]{1,0:T(8,128)S(1)} %copy-done.7, f32[128,1024]{1,0:T(8,128)S(1)} %fusion.28, ...), kind=kOutput, calls=%fused_computation.3 | convolution fusion | flops 5642387456 | bytes 13107200 | tf_op jit(solution)/shard_map/dot_general | solution.py:18
  (49 shorter events, 2.6 us)
Async XLA Ops:
  7.2 31.4 %all-gather.2.cloned.1.call-start = ((), (), s32[]{:S(2)}) async-start(), calls=%async_computation | async-start | bytes 2064384 | tf_op jit(solution)/shard_map/all_gather | solution.py:38
  7.9 195.7 %all-reduce.5.cloned.1.call-start = ((), (), s32[]{:S(2)}) async-start(), calls=%async_computation.1 | async-start | bytes 4194304 | tf_op jit(solution)/shard_map/psum | solution.py:39
  48.9 225.8 %all-reduce.7.cloned.1.call-start = ((), (), s32[]{:S(2)}) async-start(), calls=%async_computation.2 | async-start | bytes 2097152 | tf_op jit(solution)/shard_map/psum | solution.py:40
  210.3 299.4 %all-reduce.9.cloned.1.call-start = ((), (), s32[]{:S(2)}) async-start(), calls=%async_computation.3 | async-start | bytes 3670016 | tf_op jit(solution)/shard_map/psum | solution.py:43
  274.7 1.7 copy-start.10
  276.6 1.0 copy-start.11
  325.3 94.5 %copy-start.2 = (f32[1024,512]{1,0:T(8,128)S(1)}, f32[1024,512]{1,0:T(8,128)}, u32[]{:S(2)}) copy-start(f32[1024,512]{1,0:T(8,128)} %all-reduce.5.cloned.1.call-done) | copy-start | bytes 6291460
  422.9 8.9 %copy-start.3 = (bf16[1024,896]{1,0:T(8,128)(2,1)S(1)}, bf16[1024,896]{1,0:T(8,128)(2,1)}, u32[]{:S(2)}) copy-start(bf16[1024,896]{1,0:T(8,128)(2,1)} %param.4) | copy-start | bytes 5505028
  426.5 4.5 copy-start.6
  426.5 5.3 copy-start
  431.0 0.8 copy-start.8
  509.7 77.0 %copy-start.5 = (f32[512,896]{1,0:T(8,128)S(1)}, f32[512,896]{1,0:T(8,128)}, u32[]{:S(2)}) copy-start(f32[512,896]{1,0:T(8,128)} %all-reduce.9.cloned.1.call-done) | copy-start | bytes 5505028
  586.6 1.0 copy-start.7
  586.6 1.2 copy-start.9
  587.8 8.7 %copy-start.1 = (f32[1024,896]{1,0:T(8,128)S(1)}, f32[1024,896]{1,0:T(8,128)}, u32[]{:S(2)}) copy-start(f32[1024,896]{1,0:T(8,128)} %param.3) | copy-start | bytes 11010052
  587.8 8.7 %copy-start.4 = (bf16[1024,896]{1,0:T(8,128)(2,1)S(1)}, bf16[1024,896]{1,0:T(8,128)(2,1)}, u32[]{:S(2)}) copy-start(bf16[1024,896]{1,0:T(8,128)(2,1)} %param.4) | copy-start | bytes 5505028
Sparse Core Ops, SparseCore 0:
  9.8 28.6 all-gather.1
  49.0 154.4 all-reduce.4
  210.4 64.2 all-reduce.6
  440.3 69.2 all-reduce.8
where the time goes:
time: 618 us; the launch traced here: 612 us
  waiting for transfers between devices  320 us (52%)
  other arithmetic  122 us (20%)
  blocking collectives  75.1 us (12%)
  matrix products  59 us (10%)
  local copies, waits for them, and re-layouts  19.1 us (3%)
  between operations  16.8 us (3%)
    psum x1, waiting for transfers between devices, per_device(): left = lax.psum(against(combined, whole_factor), 'tp')  155 us
    another operation x14, other arithmetic, orthonormal(): lower = jnp.linalg.cholesky(gram)  78.8 us
    psum x1, blocking collectives, per_device(): squared = lax.psum(jnp.sum(right * right, axis=1), 'tp')  75.1 us
    psum x1, waiting for transfers between devices, per_device(): right = lax.psum(product(orth.T, combined), 'fsdp')  69.4 us
    psum x1, waiting for transfers between devices, per_device(): gram = lax.psum(product(left.T, left), 'fsdp')  64.2 us
    another operation x3, other arithmetic, orthonormal(): return jax.scipy.linalg.solve_triangular(lower, left.T, lower=True).T  41.4 us
    dot_general x4, matrix products, product(): jnp.dot(left, right, precision=lax.Precision.HIGHEST, preferred_element_t...  32.1 us
    all_gather x1, waiting for transfers between devices, per_device(): whole_factor = lax.all_gather(right_factor, 'fsdp', axis=0, tiled=True)  30.6 us
  transfers between devices with their start and end apart: 4, of which 4 were waited for; matrix products, arithmetic and copies ran while one was open for 0% of the time, Pallas kernels for 0%

commit v1 on v0

v1 whole, which is shorter than its diff:
```python
import functools
import math

import jax
import jax.numpy as jnp
from jax import lax
from jax.experimental import pallas as pl
from jax.experimental.pallas import tpu as pltpu
from jax.sharding import Mesh
from jax.sharding import PartitionSpec as P

D = 8192
FF = 28672
RANK = 512

decay_rest = 0.05
epsilon = 1e-06

SIZES = {"x": 4, "c": 2, "y": 4, "z": 8}
ROWS = ("x", "c")
COLS = ("y", "z")

CLOSE = 5e-3
MOST_STEPS = 9

TILE = 128


def shift(a, axis, k):
    n = SIZES[axis]
    return lax.ppermute(a, axis, [(i, (i + k) % n) for i in range(n)])


def block_of(a, index, rows):
    return lax.dynamic_slice_in_dim(a, index * rows, rows, 0)


def summed_z(a):
    spread = call(spread_kernel, (exchange(a, "z"),), f32(*a.shape), [], name="spread")
    return exchange(spread, "z")


def exchange(a, axes):
    return lax.all_to_all(a, axes, split_axis=0, concat_axis=0, tiled=True)


def relative(a, axis):
    return [a] + [shift(a, axis, k) for k in range(1, SIZES[axis])]


def split(a):
    high = a.astype(jnp.bfloat16)
    return high, (a - high.astype(jnp.float32)).astype(jnp.bfloat16)


def dot3(a, b, contract=(1, 0)):
    (ah, al), (bh, bl) = a, b
    dims = (((contract[0],), (contract[1],)), ((), ()))
    n = ah.shape[0]
    both = lax.dot_general(jnp.concatenate([ah, al]), bh, dims, preferred_element_type=jnp.float32)
    return both[:n] + (both[n:] + lax.dot_general(ah, bl, dims, preferred_element_type=jnp.float32))


def dot1(a, b, contract=(1, 0)):
    return lax.dot_general(
        a[0], b[0], (((contract[0],), (contract[1],)), ((), ())), preferred_element_type=jnp.float32
    )


def spread_kernel(parts_ref, out_ref):
    rows = parts_ref.shape[0] // SIZES["z"]
    total = parts_ref[:rows]
    for i in range(1, SIZES["z"]):
        total = total + parts_ref[i * rows : (i + 1) * rows]
    for i in range(SIZES["z"]):
        out_ref[i * rows : (i + 1) * rows] = total


def join_kernel(*refs):
    parts, out_ref = refs[:-1], refs[-1]
    n = parts[0].shape[0]
    out_ref[:n] = parts[0][...] + parts[1][...] + parts[2][...]
    out_ref[n:] = parts[3][...] + parts[4][...] + parts[5][...]


def combine_kernel(momentum_ref, gradient_ref, high_ref, low_ref):
    high_ref[...], low_ref[...] = split(momentum_ref[...] + gradient_ref[...].astype(jnp.float32))


def left_kernel(order_ref, y_ref, *refs):
    blocks, (high_ref, low_ref), outs, (factor_ref, left_ref) = refs[:8], refs[8:10], refs[10:18], refs[18:]
    rows = blocks[0].shape[0]
    for i, block in enumerate(blocks):
        factor_ref[pl.ds(pl.multiple_of(order_ref[i] * rows, rows), rows)] = block[...]
    factor = split(factor_ref[...].T)
    n = outs[0].shape[0]
    for i in range(4):
        at = slice(2 * i * n, 2 * (i + 1) * n)
        left_ref[at] = dot3((high_ref[at], low_ref[at]), factor)
    for k, out in enumerate(outs):
        out[...] = left_ref[pl.ds(pl.multiple_of(lax.rem(2 * y_ref[0] + k, 8) * n, n), n)]


def gram_kernel(band_ref, packed_ref):
    band = band_ref[...]
    across, down = split(band.T), split(band)
    at = 0
    for i in range(RANK // TILE):
        product = dot3(
            tuple(p[i * TILE : (i + 1) * TILE] for p in across), tuple(p[:, : (i + 1) * TILE] for p in down)
        )
        for j in range(i + 1):
            packed_ref[at : at + TILE] = product[:, j * TILE : (j + 1) * TILE]
            at += TILE


def absorb_kernel(places, accumulate, place_ref, *refs):
    n = len(places)
    bands, (high_ref, low_ref), refs = refs[:n], refs[n : n + 2], refs[n + 2 :]
    before, halves = (refs[:2], refs[2:]) if accumulate else (None, refs)
    c, y = place_ref[0], place_ref[1]
    h, own = RANK // 2, RANK // 8
    tiles = high_ref.shape[1] // TILE
    for p, half in enumerate(halves):
        core = 1 - c if p == 0 else c
        total = None
        for band_ref, (k, first) in zip(bands, places):
            ranks = split(band_ref[:, pl.ds(pl.multiple_of(core * h, h), h)].T)
            start = lax.rem(y + 4 - k, 4) * (high_ref.shape[0] // 4) + first
            rows = pl.ds(pl.multiple_of(start, TILE), band_ref.shape[0])
            term = dot3(ranks, (high_ref[rows], low_ref[rows]))
            total = term if total is None else total + term
        for i in range(4):
            for j in range(tiles):
                at = (i * tiles + j) * own
                piece = total[i * own : (i + 1) * own, j * TILE : (j + 1) * TILE]
                half[at : at + own] = piece + before[p][at : at + own] if accumulate else piece


def settle_kernel(*refs):
    total = refs[0][...]
    for a in refs[1:-1]:
        total = total + a[...]
    refs[-1][...] = total


def unpack(packed_ref, gram_ref):
    at = 0
    for i in range(RANK // TILE):
        for j in range(i + 1):
            block = packed_ref[at : at + TILE]
            rows, columns = slice(i * TILE, (i + 1) * TILE), slice(j * TILE, (j + 1) * TILE)
            gram_ref[rows, columns] = block
            if i != j:
                gram_ref[columns, rows] = block.T
            at += TILE


def eliminate(gram_ref, inverse_ref):
    n = gram_ref.shape[0]
    row = lax.broadcasted_iota(jnp.int32, (n, n), 0)
    column = lax.broadcasted_iota(jnp.int32, (n, n), 1)
    inverse_ref[...] = (row == column).astype(jnp.float32)

    def step(j, _):
        gram, inverse = gram_ref[...], inverse_ref[...]
        below = lax.broadcasted_iota(jnp.int32, (n, 1), 0)
        pivot_row = jnp.sum(jnp.where(row == j, gram, 0.0), axis=0, keepdims=True)
        pivot_inverse = jnp.sum(jnp.where(row == j, inverse, 0.0), axis=0, keepdims=True)
        pivot = jnp.sum(jnp.where(column[:1] == j, pivot_row, 0.0), axis=1, keepdims=True)
        scale = 1.0 / jnp.sqrt(pivot)
        factor = jnp.sum(jnp.where(column == j, gram, 0.0), axis=1, keepdims=True) * scale
        factor = jnp.where(below > j, factor, 0.0)
        gram_ref[...] = gram - factor * (pivot_row * scale)
        inverse = inverse - factor * (pivot_inverse * scale)
        inverse_ref[...] = jnp.where(row == j, pivot_inverse * scale, inverse)
        return 0

    lax.fori_loop(0, n, step, 0)


def inverse_factor_kernel(order_ref, *refs):
    blocks, (inverse_ref, packed_ref, gram_ref, w_ref) = refs[:8], refs[8:]
    n, h = RANK, RANK // 2
    rows = blocks[0].shape[0]
    for i, block in enumerate(blocks):
        packed_ref[pl.ds(pl.multiple_of(order_ref[i] * rows, 8), rows)] = block[...]
    unpack(packed_ref, gram_ref)
    row = lax.broadcasted_iota(jnp.int32, (n, n), 0)
    column = lax.broadcasted_iota(jnp.int32, (n, n), 1)
    eye = (row == column).astype(jnp.float32)
    keep = jnp.where(row > column, 1.0, 0.5 * eye)
    gram = gram_ref[...]
    diagonal = gram * eye
    by_row = lax.rsqrt(jnp.sum(diagonal, axis=1, keepdims=True))
    by_column = lax.rsqrt(jnp.sum(diagonal, axis=0, keepdims=True))
    scaled = gram * by_row * by_column
    w_ref[...] = eye - (scaled - eye) * keep
    top, low = split(scaled)
    a11, a12, a21, a22 = (
        (top[r, c], low[r, c]) for r in (slice(0, h), slice(h, n)) for c in (slice(0, h), slice(h, n))
    )
    eye_h, keep_h = eye[:h, :h], keep[:h, :h]

    def more(state):
        step, residual = state
        return jnp.logical_and(step < MOST_STEPS, jnp.logical_not(residual < CLOSE))

    def update(state, product=dot3):
        step, _ = state
        w11, w21, w22 = split(w_ref[:h, :h]), split(w_ref[h:, :h]), split(w_ref[h:, h:])
        t11 = split(product(w11, a11))
        t21 = split(product(w21, a11) + product(w22, a21))
        t22 = split(product(w21, a12) + product(w22, a22))
        e11 = product(t11, w11, (1, 1)) - eye_h
        e21 = product(t21, w11, (1, 1))
        e22 = product(t21, w21, (1, 1)) + product(t22, w22, (1, 1)) - eye_h
        p11, p21, p22 = split(e11 * keep_h), split(e21), split(e22 * keep_h)
        w_ref[:h, :h] = w_ref[:h, :h] - dot1(p11, w11)
        w_ref[h:, :h] = w_ref[h:, :h] - (dot1(p21, w11) + dot1(p22, w21))
        w_ref[h:, h:] = w_ref[h:, h:] - dot1(p22, w22)
        return step + 1, jnp.sqrt(jnp.sum(e11 * e11) + 2.0 * jnp.sum(e21 * e21) + jnp.sum(e22 * e22))

    start = update((jnp.int32(0), None), dot1)
    _, residual = lax.while_loop(more, update, (start[0], jnp.float32(1.0)))
    inverse_ref[...] = w_ref[...] * by_column

    @pl.when(jnp.logical_not(residual < CLOSE))
    def _():
        eliminate(gram_ref, inverse_ref)


def orth_kernel(y_ref, inverse_ref, *refs):
    bands, out_ref = refs[:-1], refs[-1]
    inverse = split(inverse_ref[...])
    n = out_ref.shape[0] // 4
    for band, (k, first) in zip(bands, ((0, 0), (1, 0), (2, 0), (2, n // 2), (3, 0))):
        at = pl.ds(pl.multiple_of(lax.rem(y_ref[0] + 4 - k, 4) * n + first, TILE), band.shape[0])
        out_ref[at] = dot3(split(band[...]), inverse, (1, 1))


def right_kernel(order_ref, *refs):
    blocks, (inverse_ref, right_ref, squared_ref, crossed_ref) = refs[:8], refs[8:]
    rows, h = RANK // 8, RANK // 2
    for i, block in enumerate(blocks):
        at = pl.ds(pl.multiple_of(order_ref[i] * rows, rows), rows)
        for j in range(right_ref.shape[1] // TILE):
            crossed_ref[at, j * TILE : (j + 1) * TILE] = block[j * rows : (j + 1) * rows]
    crossed = split(crossed_ref[...])
    inverse = split(inverse_ref[...])
    right_ref[:h] = dot3(tuple(p[:h, :h] for p in inverse), tuple(p[:h] for p in crossed))
    right_ref[h:] = dot3(tuple(p[h:] for p in inverse), crossed)
    right = right_ref[...]
    total = right[:, :TILE] * right[:, :TILE]
    for j in range(1, right.shape[1] // TILE):
        piece = right[:, j * TILE : (j + 1) * TILE]
        total = total + piece * piece
    sums = jnp.sum(total.T, axis=0, keepdims=True)
    for i in range(RANK // TILE):
        squared_ref[:, i, :] = jnp.broadcast_to(sums[:, i * TILE : (i + 1) * TILE], (squared_ref.shape[0], TILE))


def momentum_kernel(momentum_ref, gradient_ref, orth_ref, right_ref, out_ref, right_low):
    @pl.when(pl.program_id(0) == 0)
    def _():
        right_low[...] = right_ref[...].astype(jnp.bfloat16)

    product = jnp.dot(orth_ref[...].astype(jnp.bfloat16), right_low[...], preferred_element_type=jnp.float32)
    out_ref[...] = (momentum_ref[...] + gradient_ref[...].astype(jnp.float32)) - decay_rest * product


def update_kernel(place_ref, squared_ref, orth_ref, right_ref, update_ref, factor_ref, split_ref):
    squared = jnp.sum(squared_ref[...], axis=0)
    over = 1.0 / jnp.sqrt(squared + epsilon)
    over = jnp.concatenate([over[i : i + 1] for i in range(RANK // TILE)], axis=1)

    @pl.when(pl.program_id(0) == 0)
    def _():
        split_ref[0], split_ref[1] = split(right_ref[...])
        rows = factor_ref.shape[0]
        at = pl.multiple_of(place_ref[0] * rows, 8)
        row = lax.broadcasted_iota(jnp.int32, (rows, RANK), 0)
        column = lax.broadcasted_iota(jnp.int32, (rows, RANK), 1)
        own = jnp.sum(jnp.where(column == row + at, jnp.broadcast_to(over, (rows, RANK)), 0.0), axis=1, keepdims=True)
        factor_ref[...] = right_ref[pl.ds(at, rows)] * own

    orth = split(orth_ref[...] * over)
    update_ref[...] = (math.sqrt(D * FF / RANK) * dot3(orth, (split_ref[0], split_ref[1]))).astype(jnp.bfloat16)


def in_hbm(a):
    return pltpu.with_memory_space_constraint(a, pltpu.HBM)


def in_vmem(a):
    return pltpu.with_memory_space_constraint(a, pltpu.VMEM)


VMEM_BYTES = 20 * 2**20
VMEM, SMEM = pl.BlockSpec(memory_space=pltpu.VMEM), pl.BlockSpec(memory_space=pltpu.SMEM)


def call(kernel, given, out, scratch=(), name=None, flops=10**9):
    return pl.pallas_call(
        kernel,
        out_shape=out,
        in_specs=[SMEM if a.dtype == jnp.int32 else VMEM for a in given],
        out_specs=jax.tree.map(lambda _: VMEM, out),
        scratch_shapes=list(scratch),
        compiler_params=pltpu.CompilerParams(vmem_limit_bytes=VMEM_BYTES),
        cost_estimate=pl.CostEstimate(flops=flops, bytes_accessed=2**22, transcendentals=0),
        name=name,
    )(*given)


def f32(*shape):
    return jax.ShapeDtypeStruct(shape, jnp.float32)


def by_rows(kernel, given, out, scratch=(), name=None, flops=10**9):
    n = D // 8

    def spec(a):
        if a.shape[0] == n:
            return pl.BlockSpec((n // 4, a.shape[1]), lambda i: (i, 0))
        if a.dtype == jnp.int32:
            return SMEM
        return pl.BlockSpec(a.shape, lambda i: (0,) * len(a.shape))

    return pl.pallas_call(
        kernel,
        grid=(4,),
        out_shape=out,
        in_specs=[spec(a) for a in given],
        out_specs=jax.tree.map(spec, out),
        scratch_shapes=list(scratch),
        compiler_params=pltpu.CompilerParams(vmem_limit_bytes=VMEM_BYTES),
        cost_estimate=pl.CostEstimate(flops=flops, bytes_accessed=2**23, transcendentals=0),
        name=name,
    )(*given)


def per_device(momentum, gradient, right_factor):
    x, c, y = lax.axis_index("x"), lax.axis_index("c"), lax.axis_index("y")
    rows, columns = momentum.shape[0] // SIZES["y"], momentum.shape[1]
    wide = jax.ShapeDtypeStruct(momentum.shape, jnp.bfloat16)
    combined = by_rows(combine_kernel, (momentum, gradient), (wide, wide), name="combine")

    factor = relative(right_factor, "x")
    factor, combined = lax.optimization_barrier((factor, combined))
    factor = factor + [shift(b, "c", 1) for b in factor]
    order = jnp.stack([((x - k) % 4) * 2 + p for p in (c, 1 - c) for k in range(4)])
    terms = call(
        left_kernel,
        (order, y[None], *factor, *map(in_vmem, combined)),
        [f32(rows // 2, RANK)] * 8,
        [pltpu.VMEM((RANK, columns), jnp.float32), pltpu.VMEM((4 * rows, RANK), jnp.float32)],
        "left",
    )
    by_next, by_last = shift(terms[4], "y", 1), shift(terms[5], "y", 3)
    plain = shift(terms[3], "y", 1), shift(terms[6], "y", 3)
    passed = shift(terms[2] + by_next, "y", 1), shift(terms[7] + by_last, "y", 3)
    band = call(
        join_kernel, (terms[0], passed[0], plain[1], terms[1], plain[0], passed[1]), f32(rows, RANK), name="join"
    )
    band = summed_z(band)
    behind, ahead = shift(band, "y", 1), shift(band, "y", 3)
    across = shift(ahead[: rows // 2], "y", 3), shift(behind[rows // 2 :], "y", 1)

    place = jnp.stack([c, y])
    own, eighth = RANK // 8 * (columns // TILE), 10 * TILE // 8
    packed_rows, half = f32(10 * TILE, TILE), f32(4 * own, TILE)
    packed = call(gram_kernel, (band,), packed_rows, name="gram")

    def absorb(name, pieces, before):
        return call(
            functools.partial(absorb_kernel, [p[1:] for p in pieces], before is not None),
            (place, *[p[0] for p in pieces], *map(in_vmem, combined), *(before or ())),
            (half, half),
            name="absorb_" + name,
        )

    def exchanged(sent, kept):
        n = sent.shape[0] // 4
        came = shift(sent, "c", 1)
        return [block_of(came, (x + k) % 4, n) + block_of(kept, (x + k) % 4, n) for k in range(4)]

    def settled(parts, name):
        terms = [parts[0]] + [shift(parts[k], "x", k) for k in range(1, 4)]
        return call(settle_kernel, terms, f32(*parts[0].shape), name="settle_" + name)

    own_band, packed = lax.optimization_barrier((band, packed))
    halves = absorb("own", ((own_band, 0, 0),), None)
    parts = exchanged(block_of(packed, 1 - c, 4 * eighth), block_of(packed, c, 4 * eighth))
    parts, halves = lax.optimization_barrier((parts, halves))
    halves = absorb("near", ((behind, 1, 0), (ahead, 3, 0)), halves)
    packed = settled(parts, "gram")
    packed = call(settle_kernel, relative(packed, "y"), f32(eighth, TILE), name="settle_gram_y")
    packed, halves = lax.optimization_barrier((packed, halves))
    halves = absorb("far", ((across[0], 2, 0), (across[1], 2, rows // 2)), halves)
    packed = relative(packed, "x")
    parts = exchanged(*halves)
    parts, packed = lax.optimization_barrier((parts, packed))
    packed = packed + [shift(b, "c", 1) for b in packed]
    order = jnp.stack([p * 4 + (x - k) % 4 for p in (c, 1 - c) for k in range(4)])
    inverse = call(
        inverse_factor_kernel,
        (order, *packed),
        f32(RANK, RANK),
        [pltpu.VMEM((10 * TILE, TILE), jnp.float32)] + [pltpu.VMEM((RANK, RANK), jnp.float32)] * 2,
        name="inverse_factor",
    )
    terms = [parts[0]] + [shift(parts[k], "x", k) for k in range(1, 4)]
    terms, inverse = lax.optimization_barrier((terms, inverse))
    crossed = relative(call(settle_kernel, terms, f32(own, TILE), name="settle_crossed"), "x")
    orth = call(orth_kernel, (y[None], inverse, band, behind, *across, ahead), f32(momentum.shape[0], RANK), name="orth")
    crossed, orth = lax.optimization_barrier((crossed, orth))
    crossed = crossed + [shift(b, "c", 1) for b in crossed]
    right, squared = call(
        right_kernel,
        (order, *crossed, inverse),
        (f32(RANK, columns), f32(32, RANK // TILE, TILE)),
        [pltpu.VMEM((RANK, columns), jnp.float32)],
        "right",
    )
    right = in_hbm(right)
    squared = exchange(squared, COLS)
    new_momentum = by_rows(
        momentum_kernel,
        (in_hbm(momentum), in_hbm(gradient), orth, right),
        f32(*momentum.shape),
        [pltpu.VMEM((RANK, columns), jnp.bfloat16)],
        "momentum",
    )
    squared, new_momentum = lax.optimization_barrier((squared, new_momentum))
    update, new_factor = by_rows(
        update_kernel,
        ((x * 2 + c)[None], squared, orth, right),
        (wide, f32(*right_factor.shape)),
        [pltpu.VMEM((2, RANK, columns), jnp.bfloat16)],
        "update",
    )
    return (new_momentum, update, new_factor)


def solution(mesh):
    split_mesh = Mesh(mesh.devices.reshape(tuple(SIZES.values())), tuple(SIZES))
    spec = P(ROWS, COLS)
    return jax.shard_map(
        per_device, mesh=split_mesh, in_specs=(spec, spec, spec), out_specs=(spec, spec, spec), check_vma=False
    )
```

time: 618 us -> 560 us (0.906)
  Pallas kernels: 0 us -> 402 us
  waiting for transfers between devices: 320 us -> 53.3 us
  other arithmetic: 122 us -> 3.37 us
  matrix products: 59 us -> 0 us
  starting transfers between devices: 0.34 us -> 52 us
  blocking collectives: 75.1 us -> 25.3 us
  between operations: 16.8 us -> 1.34 us
  local copies, waits for them, and re-layouts: 19.1 us -> 11.8 us
    pallas_call x0 -> x16, Pallas kernels: none -> 402 us  [the longest x13 388 us: call(): pl.pallas_call(kernel, out_shape=out, in_specs=[SMEM if a.dtype == jnp.in...]
    psum x3 -> x0, waiting for transfers between devices: 288 us -> none  [the longest x1 155 us: per_device(): left = lax.psum(against(combined, whole_factor), 'tp')]
    another operation x17 -> x1, other arithmetic: 120 us -> 0.07 us  [per_device(): place = jnp.stack([c, y])]
    psum x1 -> x0, blocking collectives: 75.1 us -> none  [per_device(): squared = lax.psum(jnp.sum(right * right, axis=1), 'tp')]
    ppermute x0 -> x42, starting transfers between devices: none -> 44.5 us  [shift(): return lax.ppermute(a, axis, [(i, (i + k) % n) for i in range(n)])]
    dot_general x5 -> x0, matrix products: 42.4 us -> none  [the longest x4 32.1 us: product(): jnp.dot(left, right, precision=lax.Precision.HIGHEST, preferred_element_t...]
    ppermute x0 -> x42, waiting for transfers between devices: none -> 34.3 us  [shift(): return lax.ppermute(a, axis, [(i, (i + k) % n) for i in range(n)])]
    all_gather x1 -> x0, waiting for transfers between devices: 30.6 us -> none  [per_device(): whole_factor = lax.all_gather(right_factor, 'fsdp', axis=0, tiled=True)]
  transfers between devices with their start and end apart: 4 -> 44, of which waited for: 4 -> 25; matrix products, arithmetic and copies ran while one was open for 0% -> 1% of each run, Pallas kernels for 0% -> 70%
where the time goes in v1:
time: 560 us; the launch traced here: 550 us
  Pallas kernels  402 us (72%)
  waiting for transfers between devices  53.3 us (10%)
  starting transfers between devices  52 us (9%)
  blocking collectives  25.3 us (5%)
  local copies, waits for them, and re-layouts  11.8 us (2%)
    pallas_call x13, Pallas kernels, call(): pl.pallas_call(kernel, out_shape=out, in_specs=[SMEM if a.dtype == jnp.in...  388 us
    ppermute x42, starting transfers between devices, shift(): return lax.ppermute(a, axis, [(i, (i + k) % n) for i in range(n)])  44.5 us
    ppermute x42, waiting for transfers between devices, shift(): return lax.ppermute(a, axis, [(i, (i + k) % n) for i in range(n)])  34.3 us
    all_to_all x1, blocking collectives, exchange(): return lax.all_to_all(a, axes, split_axis=0, concat_axis=0, tiled=True)  25.3 us
    all_to_all x2, waiting for transfers between devices, exchange(): return lax.all_to_all(a, axes, split_axis=0, concat_axis=0, tiled=True)  19.1 us
    pallas_call x3, Pallas kernels, by_rows(): pl.pallas_call(kernel, grid=(4,), out_shape=out, in_specs=[spec(a) for a...  14.1 us
  transfers between devices with their start and end apart: 44, of which 25 were waited for; matrix products, arithmetic and copies ran while one was open for 1% of the time, Pallas kernels for 70%

profile of v1, /device:TPU:0, one launch (start us, length us, event | category | flops | bytes accessed | tf_op | source)
XLA Modules:
  0.0 549.7 jit_solution(12360867127079481943)
XLA Ops:
  0.7 2.5 collective-permute-start.1
  3.2 1.4 collective-permute-start.2
  4.6 2.0 copy-done.4
  6.7 1.5 copy-done.6
  9.0 1.2 copy-done
  10.2 3.4 collective-permute-done.1.refs_2_
  16.2 1.5 copy-done.1
  17.7 4.8 left.1
  22.5 1.7 collective-permute-start.7
  24.2 1.7 collective-permute-start.11
  25.9 1.8 collective-permute-start.9
  27.9 5.1 collective-permute-done.7
  33.5 3.1 collective-permute-start.12
  36.6 2.4 collective-permute-done.9.refs_2_
  39.0 4.5 collective-permute-done.8.refs_1_
  43.6 25.3 %all_to_all.27 = f32[8,32,512]{2,1,0:T(8,128)S(1)} all-to-all(f32[8,32,512]{2,1,0:T(8,128)S(1)} %bitcast.28), channel_id=1, replica_groups=mesh['x'=4,'c'=2,'y'=4,'z'=8] {'z'}, dimensions={0} | all-to-all | bytes 1048576 | tf_op jit(solution)/shard_map/all_to_all | solution.py:44
  69.8 3.5 all-to-all-start.1
  73.3 15.4 %all-to-all-done.1 = f32[8,32,512]{2,1,0:T(8,128)S(1)} async-done(((f32[8,32,512]{2,1,0:T(8,128)}), f32[8,32,512]{2,1,0:T(8,128)S(1)}, u32[]{:S(2)}, u32[]{:S(2)}) %all-to-all-start.1) | async-done | bytes 524320 | tf_op jit(solution)/shard_map/all_to_all | solution.py:44
  90.1 2.5 collective-permute-start.13
  92.7 1.5 copy-done.2
  94.2 1.6 absorb_own.1
  95.8 1.1 dynamic-slice_add_fusion.4
  96.9 1.4 collective-permute-start.18
  98.3 2.4 collective-permute-start.19
  100.7 1.6 collective-permute-start.20
  102.2 1.2 collective-permute-done.18.refs_1_
  105.3 4.6 collective-permute-start.22
  111.6 1.8 collective-permute-start.16
  113.3 1.9 collective-permute-done.23.refs_3_
  115.3 2.9 absorb_near.1
  118.3 1.1 collective-permute-done.16.refs_1_.refs_3_
  119.4 2.7 absorb_far.1
  123.1 1.3 collective-permute-start.25
  124.3 3.0 collective-permute-start.26
  127.6 2.1 dynamic-slice_add_fusion
  129.7 2.2 collective-permute-done.26.refs_2_
  133.3 2.9 collective-permute-start.29
  138.0 368.9 %inverse_factor.1.inverse_ref.refs_8_ = f32[512,512]{1,0:T(8,128)S(1)} custom-call(s32[8]{0:T(128)S(1)} %stack.71.order_ref, f32[160,128]{1,0:T(8,128)S(1)} %settle_gram_y.1.refs_0_, f32[160,128]{1,0:T(8,128)S(1)} %collective-permute-done.25.refs_1_, f32[160,128]{1,0:T(8,128)S(1)} %collective-permute-done.26.refs_2_, ...), custom_call_target="tpu_custom_call" | custom-call | flops 1000000000 | bytes 4194304 | tf_op jit(solution)/shard_map/inverse_factor/pallas_call | solution.py:304
  507.0 1.7 collective-permute-start.35
  509.4 2.4 collective-permute-start.37
  511.7 3.1 orth.1.orth_ref
  514.9 6.2 %collective-permute-done.35.refs_1_ = f32[448,128]{1,0:T(8,128)S(1)} collective-permute-done((f32[448,128]{1,0:T(8,128)S(1)}, f32[448,128]{1,0:T(8,128)S(1)}, u32[]{:S(2)}, u32[]{:S(2)}) %collective-permute-start.35) | collective-permute-done | bytes 229408 | tf_op jit(solution)/shard_map/ppermute | solution.py:31
  524.2 2.8 right.1
  527.0 1.2 copy-done.5
  528.2 4.0 all-to-all-start.2
  532.2 6.3 %momentum.1 = f32[1024,896]{1,0:T(8,128)} custom-call(f32[1024,896]{1,0:T(8,128)} %momentum_ref.3, bf16[1024,896]{1,0:T(8,128)(2,1)} %gradient_ref.3, f32[1024,512]{1,0:T(8,128)S(1)} %orth.1.orth_ref, f32[512,896]{1,0:T(8,128)} %copy-done.5), custom_call_target="tpu_custom_call" | custom-call | flops 1000000000 | bytes 8388608 | tf_op jit(solution)/shard_map/momentum/pallas_call | solution.py:330
  538.5 3.7 all-to-all-done.2.squared_ref
  542.2 7.0 %update.1 = (bf16[1024,896]{1,0:T(8,128)(2,1)}, f32[64,896]{1,0:T(8,128)}) custom-call(s32[1]{0:T(128)} %bitcast.22.place_ref, f32[32,4,128]{2,1,0:T(4,128)S(1)} %all-to-all-done.2.squared_ref, f32[1024,512]{1,0:T(8,128)S(1)} %orth.1.orth_ref, f32[512,896]{1,0:T(8,128)} %copy-done.5), custom_call_target="tpu_custom_call" | custom-call | flops 1000000000 | bytes 8388608 | tf_op jit(solution)/shard_map/update/pallas_call | solution.py:330
  (93 shorter events, 18.5 us)
Async XLA Ops:
  0.6 9.6 %collective-permute-start = (f32[64,896]{1,0:T(8,128)}, f32[64,896]{1,0:T(8,128)S(1)}, u32[]{:S(2)}, u32[]{:S(2)}) collective-permute-start(f32[64,896]{1,0:T(8,128)} %refs_0_), channel_id=1, source_target_pairs={{0,64},{64,128},{128,192},{192,0},{1,65},{65,129},{129,193},{193,1... | collective-permute-start | bytes 688136 | tf_op jit(solution)/shard_map/ppermute | solution.py:31
  0.7 12.9 %collective-permute-start.1 = (f32[64,896]{1,0:T(8,128)}, f32[64,896]{1,0:T(8,128)S(1)}, u32[]{:S(2)}, u32[]{:S(2)}) collective-permute-start(f32[64,896]{1,0:T(8,128)} %refs_0_), channel_id=1, source_target_pairs={{0,128},{64,192},{128,0},{192,64},{1,129},{65,193},{129,1},{193,65... | collective-permute-start | bytes 688136 | tf_op jit(solution)/shard_map/ppermute | solution.py:31
  3.2 10.4 %collective-permute-start.2 = (f32[64,896]{1,0:T(8,128)}, f32[64,896]{1,0:T(8,128)S(1)}, u32[]{:S(2)}, u32[]{:S(2)}) collective-permute-start(f32[64,896]{1,0:T(8,128)} %refs_0_), channel_id=1, source_target_pairs={{0,192},{64,0},{128,64},{192,128},{1,193},{65,1},{129,65},{193,129... | collective-permute-start | bytes 688136 | tf_op jit(solution)/shard_map/ppermute | solution.py:31
  8.2 5.5 copy-start.12
  13.6 1.5 collective-permute-start.3
  13.7 1.8 collective-permute-start.4
  14.2 2.0 collective-permute-start.5
  14.2 2.0 collective-permute-start.6
  22.5 10.4 %collective-permute-start.7 = (f32[128,512]{1,0:T(8,128)S(1)}, f32[128,512]{1,0:T(8,128)S(1)}, u32[]{:S(2)}, u32[]{:S(2)}) collective-permute-start(f32[128,512]{1,0:T(8,128)S(1)} %get-tuple-element.70), channel_id=1, source_target_pairs={{0,8},{8,16},{16,24},{24,0},{1,9},{9,17},{17,25},{25,1},{2,10},{10... | collective-permute-start | bytes 786440 | tf_op jit(solution)/shard_map/ppermute | solution.py:31
  24.2 9.3 %collective-permute-start.11 = (f32[128,512]{1,0:T(8,128)S(1)}, f32[128,512]{1,0:T(8,128)S(1)}, u32[]{:S(2)}, u32[]{:S(2)}) collective-permute-start(f32[128,512]{1,0:T(8,128)S(1)} %get-tuple-element.75), channel_id=1, source_target_pairs={{0,24},{8,0},{16,8},{24,16},{1,25},{9,1},{17,9},{25,17},{2,26},{10... | collective-permute-start | bytes 786440 | tf_op jit(solution)/shard_map/ppermute | solution.py:31
  25.9 13.1 %collective-permute-start.9 = (f32[128,512]{1,0:T(8,128)S(1)}, f32[128,512]{1,0:T(8,128)S(1)}, u32[]{:S(2)}, u32[]{:S(2)}) collective-permute-start(f32[128,512]{1,0:T(8,128)S(1)} %get-tuple-element.71), channel_id=1, source_target_pairs={{0,24},{8,0},{16,8},{24,16},{1,25},{9,1},{17,9},{25,17},{2,26},{10... | collective-permute-start | bytes 786440 | tf_op jit(solution)/shard_map/ppermute | solution.py:31
  27.7 11.3 %collective-permute-start.10 = (f32[128,512]{1,0:T(8,128)S(1)}, f32[128,512]{1,0:T(8,128)S(1)}, u32[]{:S(2)}, u32[]{:S(2)}) collective-permute-start(f32[128,512]{1,0:T(8,128)S(1)} %get-tuple-element.73), channel_id=1, source_target_pairs={{0,8},{8,16},{16,24},{24,0},{1,9},{9,17},{17,25},{25,1},{2,10},{10... | collective-permute-start | bytes 786440 | tf_op jit(solution)/shard_map/ppermute | solution.py:31
  33.0 10.5 %collective-permute-start.8 = (f32[128,512]{1,0:T(8,128)S(1)}, f32[128,512]{1,0:T(8,128)S(1)}, u32[]{:S(2)}, u32[]{:S(2)}) collective-permute-start(f32[128,512]{1,0:T(8,128)S(1)} %add.215), channel_id=1, source_target_pairs={{0,8},{8,16},{16,24},{24,0},{1,9},{9,17},{17,25},{25,1},{2,10},{10... | collective-permute-start | bytes 786440 | tf_op jit(solution)/shard_map/ppermute | solution.py:31
  33.5 10.0 %collective-permute-start.12 = (f32[128,512]{1,0:T(8,128)S(1)}, f32[128,512]{1,0:T(8,128)S(1)}, u32[]{:S(2)}, u32[]{:S(2)}) collective-permute-start(f32[128,512]{1,0:T(8,128)S(1)} %add.216), channel_id=1, source_target_pairs={{0,24},{8,0},{16,8},{24,16},{1,25},{9,1},{17,9},{25,17},{2,26},{10... | collective-permute-start | bytes 786440 | tf_op jit(solution)/shard_map/ppermute | solution.py:31
  69.8 18.9 %all-to-all-start.1 = ((f32[8,32,512]{2,1,0:T(8,128)}), f32[8,32,512]{2,1,0:T(8,128)S(1)}, u32[]{:S(2)}, u32[]{:S(2)}) async-start(f32[8,32,512]{2,1,0:T(8,128)} %bitcast.20), calls=%async_computation.1 | async-start | bytes 1048576 | tf_op jit(solution)/shard_map/all_to_all | solution.py:44
  89.3 6.5 %collective-permute-start.17 = (f32[640,128]{1,0:T(8,128)S(1)}, f32[640,128]{1,0:T(8,128)}, u32[]{:S(2)}, u32[]{:S(2)}) collective-permute-start(f32[640,128]{1,0:T(8,128)S(1)} %constant_dynamic-slice_fusion), channel_id=1, source_target_pairs={{0,32},{32,0},{1,33},{33,1},{2,34},{34,2},{3,35},{35,3},{4,36},{36... | collective-permute-start | bytes 983048 | tf_op jit(solution)/shard_map/ppermute | solution.py:31
  90.1 19.9 %collective-permute-start.13 = (f32[256,512]{1,0:T(8,128)S(1)}, f32[256,512]{1,0:T(8,128)S(1)}, u32[]{:S(2)}, u32[]{:S(2)}) collective-permute-start(f32[256,512]{1,0:T(8,128)S(1)} %bitcast.24), channel_id=1, source_target_pairs={{0,24},{8,0},{16,8},{24,16},{1,25},{9,1},{17,9},{25,17},{2,26},{10... | collective-permute-start | bytes 1572872 | tf_op jit(solution)/shard_map/ppermute | solution.py:31
  92.6 18.0 %collective-permute-start.15 = (f32[256,512]{1,0:T(8,128)S(1)}, f32[256,512]{1,0:T(8,128)}, u32[]{:S(2)}, u32[]{:S(2)}) collective-permute-start(f32[256,512]{1,0:T(8,128)S(1)} %bitcast.25), channel_id=1, source_target_pairs={{0,8},{8,16},{16,24},{24,0},{1,9},{9,17},{17,25},{25,1},{2,10},{10... | collective-permute-start | bytes 1572872 | tf_op jit(solution)/shard_map/ppermute | solution.py:31
  96.9 6.5 %collective-permute-start.18 = (f32[160,128]{1,0:T(8,128)S(1)}, f32[160,128]{1,0:T(8,128)S(1)}, u32[]{:S(2)}, u32[]{:S(2)}) collective-permute-start(f32[160,128]{1,0:T(8,128)S(1)} %get-tuple-element.81), channel_id=1, source_target_pairs={{0,64},{64,128},{128,192},{192,0},{1,65},{65,129},{129,193},{193,1... | collective-permute-start | bytes 245768 | tf_op jit(solution)/shard_map/ppermute | solution.py:31
  98.3 6.0 %collective-permute-start.19 = (f32[160,128]{1,0:T(8,128)S(1)}, f32[160,128]{1,0:T(8,128)S(1)}, u32[]{:S(2)}, u32[]{:S(2)}) collective-permute-start(f32[160,128]{1,0:T(8,128)S(1)} %get-tuple-element.82), channel_id=1, source_target_pairs={{0,128},{64,192},{128,0},{192,64},{1,129},{65,193},{129,1},{193,65... | collective-permute-start | bytes 245768 | tf_op jit(solution)/shard_map/ppermute | solution.py:31
  100.7 4.4 collective-permute-start.20
  105.1 8.2 %collective-permute-start.21 = (f32[160,128]{1,0:T(8,128)S(1)}, f32[160,128]{1,0:T(8,128)S(1)}, u32[]{:S(2)}, u32[]{:S(2)}) collective-permute-start(f32[160,128]{1,0:T(8,128)S(1)} %settle_gram.1.refs_0_), channel_id=1, source_target_pairs={{0,8},{8,16},{16,24},{24,0},{1,9},{9,17},{17,25},{25,1},{2,10},{10... | collective-permute-start | bytes 245768 | tf_op jit(solution)/shard_map/ppermute | solution.py:31
  105.3 8.0 %collective-permute-start.22 = (f32[160,128]{1,0:T(8,128)S(1)}, f32[160,128]{1,0:T(8,128)S(1)}, u32[]{:S(2)}, u32[]{:S(2)}) collective-permute-start(f32[160,128]{1,0:T(8,128)S(1)} %settle_gram.1.refs_0_), channel_id=1, source_target_pairs={{0,16},{8,24},{16,0},{24,8},{1,17},{9,25},{17,1},{25,9},{2,18},{10... | collective-permute-start | bytes 245768 | tf_op jit(solution)/shard_map/ppermute | solution.py:31
  109.9 5.4 collective-permute-start.23
  109.9 8.4 %collective-permute-start.14 = (f32[128,512]{1,0:T(8,128)S(1)}, f32[128,512]{1,0:T(8,128)S(1)}, u32[]{:S(2)}, u32[]{:S(2)}) collective-permute-start(f32[128,512]{1,0:T(8,128)S(1)} %slice.8), channel_id=1, source_target_pairs={{0,24},{8,0},{16,8},{24,16},{1,25},{9,1},{17,9},{25,17},{2,26},{10... | collective-permute-start | bytes 786440 | tf_op jit(solution)/shard_map/ppermute | solution.py:31
  111.5 3.8 copy-start.3
  111.6 7.9 %collective-permute-start.16 = (f32[128,512]{1,0:T(8,128)S(1)}, f32[128,512]{1,0:T(8,128)S(1)}, u32[]{:S(2)}, u32[]{:S(2)}) collective-permute-start(f32[128,512]{1,0:T(8,128)S(1)} %slice.9), channel_id=1, source_target_pairs={{0,8},{8,16},{16,24},{24,0},{1,9},{9,17},{17,25},{25,1},{2,10},{10... | collective-permute-start | bytes 786440 | tf_op jit(solution)/shard_map/ppermute | solution.py:31
  119.4 2.7 copy-start.7
  123.1 4.5 collective-permute-start.24
  123.1 6.7 %collective-permute-start.25 = (f32[160,128]{1,0:T(8,128)S(1)}, f32[160,128]{1,0:T(8,128)S(1)}, u32[]{:S(2)}, u32[]{:S(2)}) collective-permute-start(f32[160,128]{1,0:T(8,128)S(1)} %settle_gram_y.1.refs_0_), channel_id=1, source_target_pairs={{0,64},{64,128},{128,192},{192,0},{1,65},{65,129},{129,193},{193,1... | collective-permute-start | bytes 245768 | tf_op jit(solution)/shard_map/ppermute | solution.py:31
  124.3 7.6 %collective-permute-start.26 = (f32[160,128]{1,0:T(8,128)S(1)}, f32[160,128]{1,0:T(8,128)S(1)}, u32[]{:S(2)}, u32[]{:S(2)}) collective-permute-start(f32[160,128]{1,0:T(8,128)S(1)} %settle_gram_y.1.refs_0_), channel_id=1, source_target_pairs={{0,128},{64,192},{128,0},{192,64},{1,129},{65,193},{129,1},{193,65... | collective-permute-start | bytes 245768 | tf_op jit(solution)/shard_map/ppermute | solution.py:31
  127.3 4.6 collective-permute-start.27
  131.9 4.6 collective-permute-start.31
  131.9 4.6 collective-permute-start.32
  132.4 374.5 %collective-permute-start.28 = (f32[448,128]{1,0:T(8,128)}, f32[448,128]{1,0:T(8,128)S(1)}, u32[]{:S(2)}, u32[]{:S(2)}) collective-permute-start(f32[448,128]{1,0:T(8,128)} %get-tuple-element.94), channel_id=1, source_target_pairs={{0,64},{64,128},{128,192},{192,0},{1,65},{65,129},{129,193},{193,1... | collective-permute-start | bytes 688136 | tf_op jit(solution)/shard_map/ppermute | solution.py:31
  133.3 373.7 %collective-permute-start.29 = (f32[448,128]{1,0:T(8,128)}, f32[448,128]{1,0:T(8,128)S(1)}, u32[]{:S(2)}, u32[]{:S(2)}) collective-permute-start(f32[448,128]{1,0:T(8,128)} %get-tuple-element.95), channel_id=1, source_target_pairs={{0,128},{64,192},{128,0},{192,64},{1,129},{65,193},{129,1},{193,65... | collective-permute-start | bytes 688136 | tf_op jit(solution)/shard_map/ppermute | solution.py:31
  136.1 370.8 %collective-permute-start.30 = (f32[448,128]{1,0:T(8,128)}, f32[448,128]{1,0:T(8,128)S(1)}, u32[]{:S(2)}, u32[]{:S(2)}) collective-permute-start(f32[448,128]{1,0:T(8,128)} %get-tuple-element.96), channel_id=1, source_target_pairs={{0,192},{64,0},{128,64},{192,128},{1,193},{65,1},{129,65},{193,129... | collective-permute-start | bytes 688136 | tf_op jit(solution)/shard_map/ppermute | solution.py:31
  136.5 1.3 collective-permute-start.33
  136.5 1.4 collective-permute-start.34
  506.9 4.9 copy-start.8
  507.0 14.1 %collective-permute-start.35 = (f32[448,128]{1,0:T(8,128)S(1)}, f32[448,128]{1,0:T(8,128)S(1)}, u32[]{:S(2)}, u32[]{:S(2)}) collective-permute-start(f32[448,128]{1,0:T(8,128)S(1)} %settle_crossed.1.refs_0_), channel_id=1, source_target_pairs={{0,64},{64,128},{128,192},{192,0},{1,65},{65,129},{129,193},{193,1... | collective-permute-start | bytes 688136 | tf_op jit(solution)/shard_map/ppermute | solution.py:31
  508.7 12.4 %collective-permute-start.36 = (f32[448,128]{1,0:T(8,128)S(1)}, f32[448,128]{1,0:T(8,128)S(1)}, u32[]{:S(2)}, u32[]{:S(2)}) collective-permute-start(f32[448,128]{1,0:T(8,128)S(1)} %settle_crossed.1.refs_0_), channel_id=1, source_target_pairs={{0,128},{64,192},{128,0},{192,64},{1,129},{65,193},{129,1},{193,65... | collective-permute-start | bytes 688136 | tf_op jit(solution)/shard_map/ppermute | solution.py:31
  509.4 12.3 %collective-permute-start.37 = (f32[448,128]{1,0:T(8,128)S(1)}, f32[448,128]{1,0:T(8,128)S(1)}, u32[]{:S(2)}, u32[]{:S(2)}) collective-permute-start(f32[448,128]{1,0:T(8,128)S(1)} %settle_crossed.1.refs_0_), channel_id=1, source_target_pairs={{0,192},{64,0},{128,64},{192,128},{1,193},{65,1},{129,65},{193,129... | collective-permute-start | bytes 688136 | tf_op jit(solution)/shard_map/ppermute | solution.py:31
  521.7 1.5 collective-permute-start.38
  521.7 1.8 collective-permute-start.39
  522.2 1.6 collective-permute-start.40
  522.2 2.0 collective-permute-start.41
  528.2 14.0 %all-to-all-start.2 = ((f32[32,4,128]{2,1,0:T(4,128)}), f32[32,4,128]{2,1,0:T(4,128)S(1)}, u32[]{:S(2)}, u32[]{:S(2)}) async-start(f32[32,4,128]{2,1,0:T(4,128)} %get-tuple-element.110), calls=%async_computation.2 | async-start | bytes 131072 | tf_op jit(solution)/shard_map/all_to_all | solution.py:44
  (9 other events, 12.4 us)

commit v2 on v1

--- a/solution.py
+++ b/solution.py
@@ -101,47 +101,60 @@
         out[...] = left_ref[pl.ds(pl.multiple_of(lax.rem(2 * y_ref[0] + k, 8) * n, n), n)]
 
 
-def gram_kernel(band_ref, packed_ref):
-    band = band_ref[...]
-    across, down = split(band.T), split(band)
+def absorb_kernel(shifts, accumulate, place_ref, *refs):
+    bands = []
+    for k in shifts:
+        n = 2 if k else 1
+        bands, refs = bands + [refs[:n]], refs[n:]
+    (high_ref, low_ref), refs = refs[:2], refs[2:]
+    before, refs = (refs[:2], refs[2:]) if accumulate else (None, refs)
+    halves, (packed_ref,) = refs[:2], refs[2:]
+    c, y = place_ref[0], place_ref[1]
+    h, own, eighth = RANK // 2, RANK // 8, packed_ref.shape[0] // 8
+    tiles = high_ref.shape[1] // TILE
+    block = halves[0].shape[0] // 4
+    grams = [None] * (RANK // TILE)
+    for pieces in bands:
+        band = jnp.concatenate([p[...] for p in pieces])
+        across, down = split(band.T), split(band)
+        for i in range(RANK // TILE):
+            product = dot3(
+                tuple(p[i * TILE : (i + 1) * TILE] for p in across), tuple(p[:, : (i + 1) * TILE] for p in down)
+            )
+            grams[i] = product if grams[i] is None else grams[i] + product
     at = 0
-    for i in range(RANK // TILE):
-        product = dot3(
-            tuple(p[i * TILE : (i + 1) * TILE] for p in across), tuple(p[:, : (i + 1) * TILE] for p in down)
-        )
+    for i, product in enumerate(grams):
         for j in range(i + 1):
             packed_ref[at : at + TILE] = product[:, j * TILE : (j + 1) * TILE]
             at += TILE
-
-
-def absorb_kernel(places, accumulate, place_ref, *refs):
-    n = len(places)
-    bands, (high_ref, low_ref), refs = refs[:n], refs[n : n + 2], refs[n + 2 :]
-    before, halves = (refs[:2], refs[2:]) if accumulate else (None, refs)
-    c, y = place_ref[0], place_ref[1]
-    h, own = RANK // 2, RANK // 8
-    tiles = high_ref.shape[1] // TILE
     for p, half in enumerate(halves):
         core = 1 - c if p == 0 else c
         total = None
-        for band_ref, (k, first) in zip(bands, places):
-            ranks = split(band_ref[:, pl.ds(pl.multiple_of(core * h, h), h)].T)
-            start = lax.rem(y + 4 - k, 4) * (high_ref.shape[0] // 4) + first
-            rows = pl.ds(pl.multiple_of(start, TILE), band_ref.shape[0])
+        for pieces, k in zip(bands, shifts):
+            columns = pl.ds(pl.multiple_of(core * h, h), h)
+            ranks = split(jnp.concatenate([p[:, columns] for p in pieces]).T)
+            n = high_ref.shape[0] // 4
+            rows = pl.ds(pl.multiple_of(lax.rem(y + 4 - k, 4) * n, n), n)
             term = dot3(ranks, (high_ref[rows], low_ref[rows]))
             total = term if total is None else total + term
         for i in range(4):
             for j in range(tiles):
-                at = (i * tiles + j) * own
+                at = slice(i * block + j * own, i * block + (j + 1) * own)
                 piece = total[i * own : (i + 1) * own, j * TILE : (j + 1) * TILE]
-                half[at : at + own] = piece + before[p][at : at + own] if accumulate else piece
+                half[at] = piece + before[p][at] if accumulate else piece
+            at = slice(i * block + tiles * own, (i + 1) * block)
+            piece = packed_ref[pl.ds(pl.multiple_of((core * 4 + i) * eighth, 8), eighth)]
+            half[at] = piece + before[p][at] if accumulate else piece
 
 
 def settle_kernel(*refs):
-    total = refs[0][...]
-    for a in refs[1:-1]:
+    terms, (crossed_ref, packed_ref) = refs[:-2], refs[-2:]
+    total = terms[0][...]
+    for a in terms[1:]:
         total = total + a[...]
-    refs[-1][...] = total
+    n = crossed_ref.shape[0]
+    crossed_ref[...] = total[:n]
+    packed_ref[...] = total[n:]
 
 
 def unpack(packed_ref, gram_ref):
@@ -234,25 +247,28 @@
     bands, out_ref = refs[:-1], refs[-1]
     inverse = split(inverse_ref[...])
     n = out_ref.shape[0] // 4
-    for band, (k, first) in zip(bands, ((0, 0), (1, 0), (2, 0), (2, n // 2), (3, 0))):
+    for band, (k, first) in zip(bands, ((0, 0), (1, 0), (1, n // 2), (2, 0), (2, n // 2), (3, 0), (3, n // 2))):
         at = pl.ds(pl.multiple_of(lax.rem(y_ref[0] + 4 - k, 4) * n + first, TILE), band.shape[0])
         out_ref[at] = dot3(split(band[...]), inverse, (1, 1))
 
 
-def right_kernel(order_ref, *refs):
-    blocks, (inverse_ref, right_ref, squared_ref, crossed_ref) = refs[:8], refs[8:]
+def right_kernel(order_ref, place_ref, *refs):
+    blocks, (inverse_ref, high_ref, low_ref, own_ref, squared_ref, crossed_ref, right_ref) = refs[:8], refs[8:]
     rows, h = RANK // 8, RANK // 2
+    tiles = high_ref.shape[1] // TILE
     for i, block in enumerate(blocks):
         at = pl.ds(pl.multiple_of(order_ref[i] * rows, rows), rows)
-        for j in range(right_ref.shape[1] // TILE):
+        for j in range(tiles):
             crossed_ref[at, j * TILE : (j + 1) * TILE] = block[j * rows : (j + 1) * rows]
     crossed = split(crossed_ref[...])
     inverse = split(inverse_ref[...])
     right_ref[:h] = dot3(tuple(p[:h, :h] for p in inverse), tuple(p[:h] for p in crossed))
     right_ref[h:] = dot3(tuple(p[h:] for p in inverse), crossed)
     right = right_ref[...]
+    high_ref[...], low_ref[...] = split(right)
+    own_ref[...] = right_ref[pl.ds(pl.multiple_of(place_ref[0] * rows, rows), rows)]
     total = right[:, :TILE] * right[:, :TILE]
-    for j in range(1, right.shape[1] // TILE):
+    for j in range(1, tiles):
         piece = right[:, j * TILE : (j + 1) * TILE]
         total = total + piece * piece
     sums = jnp.sum(total.T, axis=0, keepdims=True)
@@ -260,32 +276,27 @@
         squared_ref[:, i, :] = jnp.broadcast_to(sums[:, i * TILE : (i + 1) * TILE], (squared_ref.shape[0], TILE))
 
 
-def momentum_kernel(momentum_ref, gradient_ref, orth_ref, right_ref, out_ref, right_low):
-    @pl.when(pl.program_id(0) == 0)
-    def _():
-        right_low[...] = right_ref[...].astype(jnp.bfloat16)
-
-    product = jnp.dot(orth_ref[...].astype(jnp.bfloat16), right_low[...], preferred_element_type=jnp.float32)
+def momentum_kernel(momentum_ref, gradient_ref, orth_ref, right_ref, out_ref):
+    product = jnp.dot(orth_ref[...].astype(jnp.bfloat16), right_ref[...], preferred_element_type=jnp.float32)
     out_ref[...] = (momentum_ref[...] + gradient_ref[...].astype(jnp.float32)) - decay_rest * product
 
 
-def update_kernel(place_ref, squared_ref, orth_ref, right_ref, update_ref, factor_ref, split_ref):
+def update_kernel(place_ref, squared_ref, own_ref, orth_ref, high_ref, low_ref, update_ref, factor_ref):
     squared = jnp.sum(squared_ref[...], axis=0)
     over = 1.0 / jnp.sqrt(squared + epsilon)
     over = jnp.concatenate([over[i : i + 1] for i in range(RANK // TILE)], axis=1)
 
     @pl.when(pl.program_id(0) == 0)
     def _():
-        split_ref[0], split_ref[1] = split(right_ref[...])
         rows = factor_ref.shape[0]
-        at = pl.multiple_of(place_ref[0] * rows, 8)
         row = lax.broadcasted_iota(jnp.int32, (rows, RANK), 0)
         column = lax.broadcasted_iota(jnp.int32, (rows, RANK), 1)
-        own = jnp.sum(jnp.where(column == row + at, jnp.broadcast_to(over, (rows, RANK)), 0.0), axis=1, keepdims=True)
-        factor_ref[...] = right_ref[pl.ds(at, rows)] * own
+        here = column == row + place_ref[0] * rows
+        scale = jnp.sum(jnp.where(here, jnp.broadcast_to(over, (rows, RANK)), 0.0), axis=1, keepdims=True)
+        factor_ref[...] = own_ref[...] * scale
 
     orth = split(orth_ref[...] * over)
-    update_ref[...] = (math.sqrt(D * FF / RANK) * dot3(orth, (split_ref[0], split_ref[1]))).astype(jnp.bfloat16)
+    update_ref[...] = (math.sqrt(D * FF / RANK) * dot3(orth, (high_ref[...], low_ref[...]))).astype(jnp.bfloat16)
 
 
 def in_hbm(a):
@@ -300,7 +311,7 @@
 VMEM, SMEM = pl.BlockSpec(memory_space=pltpu.VMEM), pl.BlockSpec(memory_space=pltpu.SMEM)
 
 
-def call(kernel, given, out, scratch=(), name=None, flops=10**9):
+def call(kernel, given, out, scratch=(), name=None):
     return pl.pallas_call(
         kernel,
         out_shape=out,
@@ -308,7 +319,7 @@
         out_specs=jax.tree.map(lambda _: VMEM, out),
         scratch_shapes=list(scratch),
         compiler_params=pltpu.CompilerParams(vmem_limit_bytes=VMEM_BYTES),
-        cost_estimate=pl.CostEstimate(flops=flops, bytes_accessed=2**22, transcendentals=0),
+        cost_estimate=pl.CostEstimate(flops=1, bytes_accessed=1, transcendentals=0),
         name=name,
     )(*given)
 
@@ -317,25 +328,25 @@
     return jax.ShapeDtypeStruct(shape, jnp.float32)
 
 
-def by_rows(kernel, given, out, scratch=(), name=None, flops=10**9):
+def by_rows(kernel, given, out, scratch=(), name=None, steps=4):
     n = D // 8
 
     def spec(a):
         if a.shape[0] == n:
-            return pl.BlockSpec((n // 4, a.shape[1]), lambda i: (i, 0))
+            return pl.BlockSpec((n // steps, a.shape[1]), lambda i: (i, 0))
         if a.dtype == jnp.int32:
             return SMEM
         return pl.BlockSpec(a.shape, lambda i: (0,) * len(a.shape))
 
     return pl.pallas_call(
         kernel,
-        grid=(4,),
+        grid=(steps,),
         out_shape=out,
         in_specs=[spec(a) for a in given],
         out_specs=jax.tree.map(spec, out),
         scratch_shapes=list(scratch),
         compiler_params=pltpu.CompilerParams(vmem_limit_bytes=VMEM_BYTES),
-        cost_estimate=pl.CostEstimate(flops=flops, bytes_accessed=2**23, transcendentals=0),
+        cost_estimate=pl.CostEstimate(flops=1, bytes_accessed=1, transcendentals=0),
         name=name,
     )(*given)
 
@@ -352,7 +363,7 @@
     order = jnp.stack([((x - k) % 4) * 2 + p for p in (c, 1 - c) for k in range(4)])
     terms = call(
         left_kernel,
-        (order, y[None], *factor, *map(in_vmem, combined)),
+        (order, y[None], *factor, combined[0], in_hbm(combined[1])),
         [f32(rows // 2, RANK)] * 8,
         [pltpu.VMEM((RANK, columns), jnp.float32), pltpu.VMEM((4 * rows, RANK), jnp.float32)],
         "left",
@@ -364,43 +375,33 @@
         join_kernel, (terms[0], passed[0], plain[1], terms[1], plain[0], passed[1]), f32(rows, RANK), name="join"
     )
     band = summed_z(band)
-    behind, ahead = shift(band, "y", 1), shift(band, "y", 3)
-    across = shift(ahead[: rows // 2], "y", 3), shift(behind[rows // 2 :], "y", 1)
+    top, bottom = band[: rows // 2], band[rows // 2 :]
+    ahead_top, behind_bottom = shift(top, "y", 3), shift(bottom, "y", 1)
+    behind = shift(top, "y", 1), behind_bottom
+    ahead = ahead_top, shift(bottom, "y", 3)
+    across = shift(ahead_top, "y", 3), shift(behind_bottom, "y", 1)
 
     place = jnp.stack([c, y])
     own, eighth = RANK // 8 * (columns // TILE), 10 * TILE // 8
-    packed_rows, half = f32(10 * TILE, TILE), f32(4 * own, TILE)
-    packed = call(gram_kernel, (band,), packed_rows, name="gram")
-
-    def absorb(name, pieces, before):
-        return call(
-            functools.partial(absorb_kernel, [p[1:] for p in pieces], before is not None),
-            (place, *[p[0] for p in pieces], *map(in_vmem, combined), *(before or ())),
-            (half, half),
-            name="absorb_" + name,
+    block = own + eighth
+    halves = None
+    for name, shifts, pieces in (("own", (0,), (band,)), ("near", (1, 3), behind + ahead), ("far", (2,), across)):
+        halves = call(
+            functools.partial(absorb_kernel, shifts, halves is not None),
+            (place, *pieces, *map(in_vmem, combined), *(halves or ())),
+            (f32(4 * block, TILE), f32(4 * block, TILE)),
+            [pltpu.VMEM((10 * TILE, TILE), jnp.float32)],
+            "absorb_" + name,
         )
-
-    def exchanged(sent, kept):
-        n = sent.shape[0] // 4
-        came = shift(sent, "c", 1)
-        return [block_of(came, (x + k) % 4, n) + block_of(kept, (x + k) % 4, n) for k in range(4)]
-
-    def settled(parts, name):
-        terms = [parts[0]] + [shift(parts[k], "x", k) for k in range(1, 4)]
-        return call(settle_kernel, terms, f32(*parts[0].shape), name="settle_" + name)
-
-    own_band, packed = lax.optimization_barrier((band, packed))
-    halves = absorb("own", ((own_band, 0, 0),), None)
-    parts = exchanged(block_of(packed, 1 - c, 4 * eighth), block_of(packed, c, 4 * eighth))
-    parts, halves = lax.optimization_barrier((parts, halves))
-    halves = absorb("near", ((behind, 1, 0), (ahead, 3, 0)), halves)
-    packed = settled(parts, "gram")
-    packed = call(settle_kernel, relative(packed, "y"), f32(eighth, TILE), name="settle_gram_y")
-    packed, halves = lax.optimization_barrier((packed, halves))
-    halves = absorb("far", ((across[0], 2, 0), (across[1], 2, rows // 2)), halves)
+    sent, kept = halves
+    came = shift(sent, "c", 1)
+    parts = [block_of(came, (x + k) % 4, block) + block_of(kept, (x + k) % 4, block) for k in range(4)]
+    terms = [parts[0]] + [shift(parts[k], "x", k) for k in range(1, 4)]
+    crossed, packed = call(settle_kernel, terms, (f32(own, TILE), f32(eighth, TILE)), name="settle")
     packed = relative(packed, "x")
-    parts = exchanged(*halves)
-    parts, packed = lax.optimization_barrier((parts, packed))
+    near = shift(crossed, "x", 1), shift(crossed, "x", 3)
+    far, packed = lax.optimization_barrier((crossed, packed))
+    crossed = [crossed, near[0], shift(far, "x", 2), near[1]]
     packed = packed + [shift(b, "c", 1) for b in packed]
     order = jnp.stack([p * 4 + (x - k) % 4 for p in (c, 1 - c) for k in range(4)])
     inverse = call(
@@ -410,35 +411,29 @@
         [pltpu.VMEM((10 * TILE, TILE), jnp.float32)] + [pltpu.VMEM((RANK, RANK), jnp.float32)] * 2,
         name="inverse_factor",
     )
-    terms = [parts[0]] + [shift(parts[k], "x", k) for k in range(1, 4)]
-    terms, inverse = lax.optimization_barrier((terms, inverse))
-    crossed = relative(call(settle_kernel, terms, f32(own, TILE), name="settle_crossed"), "x")
-    orth = call(orth_kernel, (y[None], inverse, band, behind, *across, ahead), f32(momentum.shape[0], RANK), name="orth")
+    orth = call(orth_kernel, (y[None], inverse, *map(in_hbm, (band, *behind, *across, *ahead))), f32(momentum.shape[0], RANK), name="orth")
     crossed, orth = lax.optimization_barrier((crossed, orth))
     crossed = crossed + [shift(b, "c", 1) for b in crossed]
-    right, squared = call(
+    place = (x * 2 + c)[None]
+    half_width = jax.ShapeDtypeStruct((RANK, columns), jnp.bfloat16)
+    high, low, right, squared = call(
         right_kernel,
-        (order, *crossed, inverse),
-        (f32(RANK, columns), f32(32, RANK // TILE, TILE)),
-        [pltpu.VMEM((RANK, columns), jnp.float32)],
+        (order, place, *map(in_hbm, crossed), inverse),
+        (half_width, half_width, f32(*right_factor.shape), f32(32, RANK // TILE, TILE)),
+        [pltpu.VMEM((RANK, columns), jnp.float32)] * 2,
         "right",
     )
-    right = in_hbm(right)
     squared = exchange(squared, COLS)
     new_momentum = by_rows(
-        momentum_kernel,
-        (in_hbm(momentum), in_hbm(gradient), orth, right),
-        f32(*momentum.shape),
-        [pltpu.VMEM((RANK, columns), jnp.bfloat16)],
-        "momentum",
+        momentum_kernel, (in_hbm(momentum), in_hbm(gradient), orth, in_hbm(high)), f32(*momentum.shape), name="momentum"
     )
     squared, new_momentum = lax.optimization_barrier((squared, new_momentum))
     update, new_factor = by_rows(
         update_kernel,
-        ((x * 2 + c)[None], squared, orth, right),
+        (place, squared, right, orth, in_hbm(high), in_hbm(low)),
         (wide, f32(*right_factor.shape)),
-        [pltpu.VMEM((2, RANK, columns), jnp.bfloat16)],
-        "update",
+        name="update",
+        steps=2,
     )
     return (new_momentum, update, new_factor)
 

time: 560 us -> 541 us (0.966)
  blocking collectives: 25.3 us -> 43.8 us
  Pallas kernels: 402 us -> 386 us
  waiting for transfers between devices: 53.3 us -> 46.5 us
  starting transfers between devices: 52 us -> 45.6 us
    all_to_all x1 -> x2, blocking collectives: 25.3 us -> 43.8 us  [exchange(): return lax.all_to_all(a, axes, split_axis=0, concat_axis=0, tiled=True)]
    pallas_call x13 -> x10, Pallas kernels: 388 us -> 373 us  [call(): pl.pallas_call(kernel, out_shape=out, in_specs=[SMEM if a.dtype == jnp.in...]
    all_to_all x2 -> x1, waiting for transfers between devices: 19.1 us -> 3.87 us  [exchange(): return lax.all_to_all(a, axes, split_axis=0, concat_axis=0, tiled=True)]
    ppermute x42 -> x37, waiting for transfers between devices: 34.3 us -> 42.7 us  [shift(): return lax.ppermute(a, axis, [(i, (i + k) % n) for i in range(n)])]
    ppermute x42 -> x37, starting transfers between devices: 44.5 us -> 41.7 us  [shift(): return lax.ppermute(a, axis, [(i, (i + k) % n) for i in range(n)])]
  transfers between devices with their start and end apart: 44 -> 38, of which waited for: 25 -> 25; matrix products, arithmetic and copies ran while one was open for 1% -> 0% of each run, Pallas kernels for 70% -> 69%
where the time goes in v2:
time: 541 us; the launch traced here: 531 us
  Pallas kernels  386 us (71%)
  waiting for transfers between devices  46.5 us (9%)
  starting transfers between devices  45.6 us (8%)
  blocking collectives  43.8 us (8%)
  local copies, waits for them, and re-layouts  6.92 us (1%)
    pallas_call x10, Pallas kernels, call(): pl.pallas_call(kernel, out_shape=out, in_specs=[SMEM if a.dtype == jnp.in...  373 us
    all_to_all x2, blocking collectives, exchange(): return lax.all_to_all(a, axes, split_axis=0, concat_axis=0, tiled=True)  43.8 us
    ppermute x37, waiting for transfers between devices, shift(): return lax.ppermute(a, axis, [(i, (i + k) % n) for i in range(n)])  42.7 us
    ppermute x37, starting transfers between devices, shift(): return lax.ppermute(a, axis, [(i, (i + k) % n) for i in range(n)])  41.7 us
    pallas_call x3, Pallas kernels, by_rows(): pl.pallas_call(kernel, grid=(steps,), out_shape=out, in_specs=[spec(a) fo...  13.1 us
  transfers between devices with their start and end apart: 38, of which 25 were waited for; matrix products, arithmetic and copies ran while one was open for 0% of the time, Pallas kernels for 69%

profile of v2, /device:TPU:0, one launch (start us, length us, event | category | flops | bytes accessed | tf_op | source)
XLA Modules:
  0.0 530.6 jit_solution(5529920266643881607)
XLA Ops:
  0.7 2.5 collective-permute-start.1
  3.2 1.4 collective-permute-start.2
  4.6 2.0 copy-done.2
  6.7 1.5 copy-done.4
  8.2 0.8 combine.1
  9.0 1.2 copy-done
  10.2 3.4 collective-permute-done.1.refs_2_
  16.2 5.5 %left.1 = (f32[128,512]{1,0:T(8,128)S(1)}, f32[128,512]{1,0:T(8,128)S(1)}, f32[128,512]{1,0:T(8,128)S(1)}, f32[128,512]{1,0:T(8,128)S(1)}, f32[128,512]{1,0:T(8,...) custom-call(s32[8]{0:T(128)S(1)} %stack.83.order_ref, s32[1]{0:T(128)} %bitcast.10.y_ref, ...), custom_call_target="tpu_custom_call" | custom-call | flops 1 | bytes 1 | tf_op jit(solution)/shard_map/left/pallas_call | solution.py:315
  21.7 1.7 collective-permute-start.7
  23.4 1.7 collective-permute-start.11
  25.1 1.8 collective-permute-start.9
  27.1 5.1 collective-permute-done.7
  32.7 3.1 collective-permute-start.12
  35.8 2.4 collective-permute-done.9.refs_2_
  38.2 4.5 collective-permute-done.8.refs_1_
  42.8 25.3 %all_to_all.27 = f32[8,32,512]{2,1,0:T(8,128)S(1)} all-to-all(f32[8,32,512]{2,1,0:T(8,128)S(1)} %bitcast.29), channel_id=1, replica_groups=mesh['x'=4,'c'=2,'y'=4,'z'=8] {'z'}, dimensions={0} | all-to-all | bytes 1048576 | tf_op jit(solution)/shard_map/all_to_all | solution.py:44
  68.2 18.5 %all_to_all.28 = f32[8,32,512]{2,1,0:T(8,128)S(1)} all-to-all(f32[8,32,512]{2,1,0:T(8,128)S(1)} %bitcast.28), channel_id=1, replica_groups=mesh['x'=4,'c'=2,'y'=4,'z'=8] {'z'}, dimensions={0} | all-to-all | bytes 1048576 | tf_op jit(solution)/shard_map/all_to_all | solution.py:44
  86.8 2.7 collective-permute-start.13
  89.8 2.9 collective-permute-start.18
  92.7 3.5 collective-permute-done.13.refs_2_.refs_5_
  96.2 3.7 collective-permute-start.14
  100.0 1.9 absorb_own.1
  101.9 1.5 collective-permute-done.17.refs_0_.refs_1_
  103.5 3.1 absorb_near.1
  106.6 0.9 collective-permute-done.16.refs_1_.refs_4_
  107.5 2.5 absorb_far.1
  110.1 3.1 collective-permute-done.19
  113.3 1.4 collective-permute-start.20
  114.7 2.4 collective-permute-start.21
  117.1 1.8 collective-permute-start.22
  118.9 5.4 %collective-permute-done.20.refs_1_ = f32[608,128]{1,0:T(8,128)S(1)} collective-permute-done((f32[608,128]{1,0:T(8,128)S(1)}, f32[608,128]{1,0:T(8,128)S(1)}, u32[]{:S(2)}, u32[]{:S(2)}) %collective-permute-start.20) | collective-permute-done | bytes 311328 | tf_op jit(solution)/shard_map/ppermute | solution.py:31
  124.3 6.9 %collective-permute-done.21.refs_2_ = f32[608,128]{1,0:T(8,128)S(1)} collective-permute-done((f32[608,128]{1,0:T(8,128)S(1)}, f32[608,128]{1,0:T(8,128)S(1)}, u32[]{:S(2)}, u32[]{:S(2)}) %collective-permute-start.21) | collective-permute-done | bytes 311328 | tf_op jit(solution)/shard_map/ppermute | solution.py:31
  131.4 2.0 collective-permute-start.24
  133.4 2.2 collective-permute-start.25
  135.6 1.2 collective-permute-start.26
  136.8 0.8 collective-permute-start.23
  137.6 2.4 collective-permute-start.28
  140.9 1.5 collective-permute-start.27
  145.1 352.0 %inverse_factor.1.inverse_ref.refs_8_ = f32[512,512]{1,0:T(8,128)S(1)} custom-call(s32[8]{0:T(128)S(1)} %stack.71.order_ref, f32[160,128]{1,0:T(8,128)S(1)} %get-tuple-element.70.refs_0_, f32[160,128]{1,0:T(8,128)S(1)} %collective-permute-done.24.refs_1_, f32[160,128]{1,0:T(8,128)S(1)} %collective-permute-done.25.refs_2_, ...), custom_call_target="tpu_custom_call" | custom-call | flops 1 | bytes 1 | tf_op jit(solution)/shard_map/inverse_factor/pallas_call | solution.py:315
  497.1 3.9 orth.1.orth_ref
  502.8 0.9 collective-permute-done.34.refs_5_
  504.3 3.9 right.1
  508.2 1.0 copy-done.5
  509.2 0.9 copy-done.12
  510.1 3.9 all-to-all-start.2
  514.0 6.1 %momentum.1 = f32[1024,896]{1,0:T(8,128)} custom-call(f32[1024,896]{1,0:T(8,128)} %momentum_ref.3, bf16[1024,896]{1,0:T(8,128)(2,1)} %gradient_ref.3, f32[1024,512]{1,0:T(8,128)S(1)} %orth.1.orth_ref, bf16[512,896]{1,0:T(8,128)(2,1)} %copy-done.5), custom_call_target="tpu_custom_call" | custom-call | flops 1 | bytes 1 | tf_op jit(solution)/shard_map/momentum/pallas_call | solution.py:341
  520.1 3.9 all-to-all-done.2.squared_ref
  524.0 6.2 %update.1 = (bf16[1024,896]{1,0:T(8,128)(2,1)}, f32[64,896]{1,0:T(8,128)}) custom-call(s32[1]{0:T(128)} %bitcast.8.place_ref, f32[32,4,128]{2,1,0:T(4,128)S(1)} %all-to-all-done.2.squared_ref, f32[64,896]{1,0:T(8,128)S(1)} %get-tuple-element.83.own_ref, f32[1024,512]{1,0:T(8,128)S(1)} %orth.1.orth_ref, bf16[512,896]{1,0:T(8,128)(2,1)} %copy-done.5, ...), custom_call_target="tpu_custom_call" | custom-call | flops 1 | bytes 1 | tf_op jit(solution)/shard_map/update/pallas_call | solution.py:341
  (80 shorter events, 10.4 us)
Async XLA Ops:
  0.6 9.6 %collective-permute-start = (f32[64,896]{1,0:T(8,128)}, f32[64,896]{1,0:T(8,128)S(1)}, u32[]{:S(2)}, u32[]{:S(2)}) collective-permute-start(f32[64,896]{1,0:T(8,128)} %refs_0_), channel_id=1, source_target_pairs={{0,64},{64,128},{128,192},{192,0},{1,65},{65,129},{129,193},{193,1... | collective-permute-start | bytes 688136 | tf_op jit(solution)/shard_map/ppermute | solution.py:31
  0.7 12.9 %collective-permute-start.1 = (f32[64,896]{1,0:T(8,128)}, f32[64,896]{1,0:T(8,128)S(1)}, u32[]{:S(2)}, u32[]{:S(2)}) collective-permute-start(f32[64,896]{1,0:T(8,128)} %refs_0_), channel_id=1, source_target_pairs={{0,128},{64,192},{128,0},{192,64},{1,129},{65,193},{129,1},{193,65... | collective-permute-start | bytes 688136 | tf_op jit(solution)/shard_map/ppermute | solution.py:31
  3.2 10.4 %collective-permute-start.2 = (f32[64,896]{1,0:T(8,128)}, f32[64,896]{1,0:T(8,128)S(1)}, u32[]{:S(2)}, u32[]{:S(2)}) collective-permute-start(f32[64,896]{1,0:T(8,128)} %refs_0_), channel_id=1, source_target_pairs={{0,192},{64,0},{128,64},{192,128},{1,193},{65,1},{129,65},{193,129... | collective-permute-start | bytes 688136 | tf_op jit(solution)/shard_map/ppermute | solution.py:31
  8.2 5.5 %copy-start.13 = (f32[64,896]{1,0:T(8,128)S(1)}, f32[64,896]{1,0:T(8,128)}, u32[]{:S(2)}) copy-start(f32[64,896]{1,0:T(8,128)} %refs_0_) | copy-start | bytes 688132
  13.6 1.5 collective-permute-start.3
  13.7 1.8 collective-permute-start.4
  14.2 2.0 collective-permute-start.5
  14.2 2.0 collective-permute-start.6
  21.7 10.4 %collective-permute-start.7 = (f32[128,512]{1,0:T(8,128)S(1)}, f32[128,512]{1,0:T(8,128)S(1)}, u32[]{:S(2)}, u32[]{:S(2)}) collective-permute-start(f32[128,512]{1,0:T(8,128)S(1)} %get-tuple-element.55), channel_id=1, source_target_pairs={{0,8},{8,16},{16,24},{24,0},{1,9},{9,17},{17,25},{25,1},{2,10},{10... | collective-permute-start | bytes 786440 | tf_op jit(solution)/shard_map/ppermute | solution.py:31
  23.4 9.3 %collective-permute-start.11 = (f32[128,512]{1,0:T(8,128)S(1)}, f32[128,512]{1,0:T(8,128)S(1)}, u32[]{:S(2)}, u32[]{:S(2)}) collective-permute-start(f32[128,512]{1,0:T(8,128)S(1)} %get-tuple-element.60), channel_id=1, source_target_pairs={{0,24},{8,0},{16,8},{24,16},{1,25},{9,1},{17,9},{25,17},{2,26},{10... | collective-permute-start | bytes 786440 | tf_op jit(solution)/shard_map/ppermute | solution.py:31
  25.1 13.1 %collective-permute-start.9 = (f32[128,512]{1,0:T(8,128)S(1)}, f32[128,512]{1,0:T(8,128)S(1)}, u32[]{:S(2)}, u32[]{:S(2)}) collective-permute-start(f32[128,512]{1,0:T(8,128)S(1)} %get-tuple-element.56), channel_id=1, source_target_pairs={{0,24},{8,0},{16,8},{24,16},{1,25},{9,1},{17,9},{25,17},{2,26},{10... | collective-permute-start | bytes 786440 | tf_op jit(solution)/shard_map/ppermute | solution.py:31
  26.9 11.3 %collective-permute-start.10 = (f32[128,512]{1,0:T(8,128)S(1)}, f32[128,512]{1,0:T(8,128)S(1)}, u32[]{:S(2)}, u32[]{:S(2)}) collective-permute-start(f32[128,512]{1,0:T(8,128)S(1)} %get-tuple-element.58), channel_id=1, source_target_pairs={{0,8},{8,16},{16,24},{24,0},{1,9},{9,17},{17,25},{25,1},{2,10},{10... | collective-permute-start | bytes 786440 | tf_op jit(solution)/shard_map/ppermute | solution.py:31
  32.2 10.5 %collective-permute-start.8 = (f32[128,512]{1,0:T(8,128)S(1)}, f32[128,512]{1,0:T(8,128)S(1)}, u32[]{:S(2)}, u32[]{:S(2)}) collective-permute-start(f32[128,512]{1,0:T(8,128)S(1)} %add.160), channel_id=1, source_target_pairs={{0,8},{8,16},{16,24},{24,0},{1,9},{9,17},{17,25},{25,1},{2,10},{10... | collective-permute-start | bytes 786440 | tf_op jit(solution)/shard_map/ppermute | solution.py:31
  32.7 10.0 %collective-permute-start.12 = (f32[128,512]{1,0:T(8,128)S(1)}, f32[128,512]{1,0:T(8,128)S(1)}, u32[]{:S(2)}, u32[]{:S(2)}) collective-permute-start(f32[128,512]{1,0:T(8,128)S(1)} %add.161), channel_id=1, source_target_pairs={{0,24},{8,0},{16,8},{24,16},{1,25},{9,1},{17,9},{25,17},{2,26},{10... | collective-permute-start | bytes 786440 | tf_op jit(solution)/shard_map/ppermute | solution.py:31
  68.2 31.8 %copy-start.1 = (bf16[1024,896]{1,0:T(8,128)(2,1)S(1)}, bf16[1024,896]{1,0:T(8,128)(2,1)}, u32[]{:S(2)}) copy-start(bf16[1024,896]{1,0:T(8,128)(2,1)} %copy-done) | copy-start | bytes 5505028
  86.7 15.2 %copy-start.3 = (f32[8,32,512]{2,1,0:T(8,128)}, f32[8,32,512]{2,1,0:T(8,128)S(1)}, u32[]{:S(2)}) copy-start(f32[8,32,512]{2,1,0:T(8,128)S(1)} %all_to_all.28) | copy-start | bytes 1572868
  86.8 9.5 %collective-permute-start.13 = (f32[128,512]{1,0:T(8,128)S(1)}, f32[128,512]{1,0:T(8,128)S(1)}, u32[]{:S(2)}, u32[]{:S(2)}) collective-permute-start(f32[128,512]{1,0:T(8,128)S(1)} %bitcast.32), channel_id=1, source_target_pairs={{0,24},{8,0},{16,8},{24,16},{1,25},{9,1},{17,9},{25,17},{2,26},{10... | collective-permute-start | bytes 786440 | tf_op jit(solution)/shard_map/ppermute | solution.py:31
  89.5 10.5 %collective-permute-start.15 = (f32[128,512]{1,0:T(8,128)S(1)}, f32[128,512]{1,0:T(8,128)S(1)}, u32[]{:S(2)}, u32[]{:S(2)}) collective-permute-start(f32[128,512]{1,0:T(8,128)S(1)} %bitcast.30), channel_id=1, source_target_pairs={{0,8},{8,16},{16,24},{24,0},{1,9},{9,17},{17,25},{25,1},{2,10},{10... | collective-permute-start | bytes 786440 | tf_op jit(solution)/shard_map/ppermute | solution.py:31
  89.5 14.0 %collective-permute-start.17 = (f32[128,512]{1,0:T(8,128)S(1)}, f32[128,512]{1,0:T(8,128)S(1)}, u32[]{:S(2)}, u32[]{:S(2)}) collective-permute-start(f32[128,512]{1,0:T(8,128)S(1)} %bitcast.33), channel_id=1, source_target_pairs={{0,8},{8,16},{16,24},{24,0},{1,9},{9,17},{17,25},{25,1},{2,10},{10... | collective-permute-start | bytes 786440 | tf_op jit(solution)/shard_map/ppermute | solution.py:31
  89.8 13.6 %collective-permute-start.18 = (f32[128,512]{1,0:T(8,128)S(1)}, f32[128,512]{1,0:T(8,128)S(1)}, u32[]{:S(2)}, u32[]{:S(2)}) collective-permute-start(f32[128,512]{1,0:T(8,128)S(1)} %bitcast.31), channel_id=1, source_target_pairs={{0,24},{8,0},{16,8},{24,16},{1,25},{9,1},{17,9},{25,17},{2,26},{10... | collective-permute-start | bytes 786440 | tf_op jit(solution)/shard_map/ppermute | solution.py:31
  96.2 7.2 %copy-start.6 = (f32[128,512]{1,0:T(8,128)}, f32[128,512]{1,0:T(8,128)S(1)}, u32[]{:S(2)}) copy-start(f32[128,512]{1,0:T(8,128)S(1)} %collective-permute-done.13.refs_2_.refs_5_) | copy-start | bytes 786436
  96.2 10.4 %collective-permute-start.14 = (f32[128,512]{1,0:T(8,128)S(1)}, f32[128,512]{1,0:T(8,128)S(1)}, u32[]{:S(2)}, u32[]{:S(2)}) collective-permute-start(f32[128,512]{1,0:T(8,128)S(1)} %collective-permute-done.13.refs_2_.refs_5_), channel_id=1, source_target_pairs={{0,24},{8,0},{16,8},{24,16},{1,25},{9,1},{17,9},{25,17},{2,26},{10... | collective-permute-start | bytes 786440 | tf_op jit(solution)/shard_map/ppermute | solution.py:31
  99.9 3.5 copy-start.7
  99.9 7.6 %collective-permute-start.16 = (f32[128,512]{1,0:T(8,128)S(1)}, f32[128,512]{1,0:T(8,128)S(1)}, u32[]{:S(2)}, u32[]{:S(2)}) collective-permute-start(f32[128,512]{1,0:T(8,128)S(1)} %collective-permute-done.15.refs_1_.refs_2_), channel_id=1, source_target_pairs={{0,8},{8,16},{16,24},{24,0},{1,9},{9,17},{17,25},{25,1},{2,10},{10... | collective-permute-start | bytes 786440 | tf_op jit(solution)/shard_map/ppermute | solution.py:31
  103.4 3.1 copy-start.8
  103.4 3.1 copy-start.9
  106.6 3.5 copy-start.10
  107.5 2.5 copy-start.11
  110.1 3.2 collective-permute-start.19
  113.3 11.0 %collective-permute-start.20 = (f32[608,128]{1,0:T(8,128)S(1)}, f32[608,128]{1,0:T(8,128)S(1)}, u32[]{:S(2)}, u32[]{:S(2)}) collective-permute-start(f32[608,128]{1,0:T(8,128)S(1)} %get-tuple-element.89), channel_id=1, source_target_pairs={{0,64},{64,128},{128,192},{192,0},{1,65},{65,129},{129,193},{193,1... | collective-permute-start | bytes 933896 | tf_op jit(solution)/shard_map/ppermute | solution.py:31
  114.7 16.4 %collective-permute-start.21 = (f32[608,128]{1,0:T(8,128)S(1)}, f32[608,128]{1,0:T(8,128)S(1)}, u32[]{:S(2)}, u32[]{:S(2)}) collective-permute-start(f32[608,128]{1,0:T(8,128)S(1)} %get-tuple-element.88), channel_id=1, source_target_pairs={{0,128},{64,192},{128,0},{192,64},{1,129},{65,193},{129,1},{193,65... | collective-permute-start | bytes 933896 | tf_op jit(solution)/shard_map/ppermute | solution.py:31
  117.1 14.2 %collective-permute-start.22 = (f32[608,128]{1,0:T(8,128)S(1)}, f32[608,128]{1,0:T(8,128)S(1)}, u32[]{:S(2)}, u32[]{:S(2)}) collective-permute-start(f32[608,128]{1,0:T(8,128)S(1)} %get-tuple-element.87), channel_id=1, source_target_pairs={{0,192},{64,0},{128,64},{192,128},{1,193},{65,1},{129,65},{193,129... | collective-permute-start | bytes 933896 | tf_op jit(solution)/shard_map/ppermute | solution.py:31
  131.4 369.7 %copy-start.14 = (f32[448,128]{1,0:T(8,128)}, f32[448,128]{1,0:T(8,128)S(1)}, u32[]{:S(2)}) copy-start(f32[448,128]{1,0:T(8,128)S(1)} %get-tuple-element.74.refs_0_) | copy-start | bytes 688132
  131.4 8.6 %collective-permute-start.24 = (f32[160,128]{1,0:T(8,128)S(1)}, f32[160,128]{1,0:T(8,128)S(1)}, u32[]{:S(2)}, u32[]{:S(2)}) collective-permute-start(f32[160,128]{1,0:T(8,128)S(1)} %get-tuple-element.70.refs_0_), channel_id=1, source_target_pairs={{0,64},{64,128},{128,192},{192,0},{1,65},{65,129},{129,193},{193,1... | collective-permute-start | bytes 245768 | tf_op jit(solution)/shard_map/ppermute | solution.py:31
  133.4 7.2 %collective-permute-start.25 = (f32[160,128]{1,0:T(8,128)S(1)}, f32[160,128]{1,0:T(8,128)S(1)}, u32[]{:S(2)}, u32[]{:S(2)}) collective-permute-start(f32[160,128]{1,0:T(8,128)S(1)} %get-tuple-element.70.refs_0_), channel_id=1, source_target_pairs={{0,128},{64,192},{128,0},{192,64},{1,129},{65,193},{129,1},{193,65... | collective-permute-start | bytes 245768 | tf_op jit(solution)/shard_map/ppermute | solution.py:31
  135.6 5.3 %collective-permute-start.26 = (f32[160,128]{1,0:T(8,128)S(1)}, f32[160,128]{1,0:T(8,128)S(1)}, u32[]{:S(2)}, u32[]{:S(2)}) collective-permute-start(f32[160,128]{1,0:T(8,128)S(1)} %get-tuple-element.70.refs_0_), channel_id=1, source_target_pairs={{0,192},{64,0},{128,64},{192,128},{1,193},{65,1},{129,65},{193,129... | collective-permute-start | bytes 245768 | tf_op jit(solution)/shard_map/ppermute | solution.py:31
  136.8 364.2 %collective-permute-start.23 = (f32[448,128]{1,0:T(8,128)S(1)}, f32[448,128]{1,0:T(8,128)}, u32[]{:S(2)}, u32[]{:S(2)}) collective-permute-start(f32[448,128]{1,0:T(8,128)S(1)} %get-tuple-element.74.refs_0_), channel_id=1, source_target_pairs={{0,64},{64,128},{128,192},{192,0},{1,65},{65,129},{129,193},{193,1... | collective-permute-start | bytes 688136 | tf_op jit(solution)/shard_map/ppermute | solution.py:31
  137.6 363.4 %collective-permute-start.28 = (f32[448,128]{1,0:T(8,128)S(1)}, f32[448,128]{1,0:T(8,128)}, u32[]{:S(2)}, u32[]{:S(2)}) collective-permute-start(f32[448,128]{1,0:T(8,128)S(1)} %get-tuple-element.74.refs_0_), channel_id=1, source_target_pairs={{0,192},{64,0},{128,64},{192,128},{1,193},{65,1},{129,65},{193,129... | collective-permute-start | bytes 688136 | tf_op jit(solution)/shard_map/ppermute | solution.py:31
  140.9 360.2 %collective-permute-start.27 = (f32[448,128]{1,0:T(8,128)S(1)}, f32[448,128]{1,0:T(8,128)}, u32[]{:S(2)}, u32[]{:S(2)}) collective-permute-start(f32[448,128]{1,0:T(8,128)S(1)} %get-tuple-element.74.refs_0_), channel_id=1, source_target_pairs={{0,128},{64,192},{128,0},{192,64},{1,129},{65,193},{129,1},{193,65... | collective-permute-start | bytes 688136 | tf_op jit(solution)/shard_map/ppermute | solution.py:31
  142.4 1.3 collective-permute-start.29
  142.4 1.4 collective-permute-start.30
  143.7 1.3 collective-permute-start.31
  143.8 1.3 collective-permute-start.32
  501.0 1.7 collective-permute-start.33
  501.5 2.1 collective-permute-start.34
  502.0 2.0 collective-permute-start.35
  502.3 2.0 collective-permute-start.36
  510.1 13.9 %all-to-all-start.2 = ((f32[32,4,128]{2,1,0:T(4,128)}), f32[32,4,128]{2,1,0:T(4,128)S(1)}, u32[]{:S(2)}, u32[]{:S(2)}) async-start(f32[32,4,128]{2,1,0:T(4,128)} %get-tuple-element.78), calls=%async_computation.2 | async-start | bytes 131072 | tf_op jit(solution)/shard_map/all_to_all | solution.py:44
  (5 other events, 6.7 us)

commit v3 on v2

--- a/solution.py
+++ b/solution.py
@@ -276,8 +276,12 @@
         squared_ref[:, i, :] = jnp.broadcast_to(sums[:, i * TILE : (i + 1) * TILE], (squared_ref.shape[0], TILE))
 
 
-def momentum_kernel(momentum_ref, gradient_ref, orth_ref, right_ref, out_ref):
-    product = jnp.dot(orth_ref[...].astype(jnp.bfloat16), right_ref[...], preferred_element_type=jnp.float32)
+def momentum_kernel(momentum_ref, gradient_ref, orth_ref, high_ref, low_ref, out_ref, high_out, low_out):
+    @pl.when(pl.program_id(0) == 0)
+    def _():
+        high_out[...], low_out[...] = high_ref[...], low_ref[...]
+
+    product = jnp.dot(orth_ref[...].astype(jnp.bfloat16), high_ref[...], preferred_element_type=jnp.float32)
     out_ref[...] = (momentum_ref[...] + gradient_ref[...].astype(jnp.float32)) - decay_rest * product
 
 
@@ -345,7 +349,7 @@
         in_specs=[spec(a) for a in given],
         out_specs=jax.tree.map(spec, out),
         scratch_shapes=list(scratch),
-        compiler_params=pltpu.CompilerParams(vmem_limit_bytes=VMEM_BYTES),
+        compiler_params=pltpu.CompilerParams(vmem_limit_bytes=32 * 2**20),
         cost_estimate=pl.CostEstimate(flops=1, bytes_accessed=1, transcendentals=0),
         name=name,
     )(*given)
@@ -424,13 +428,17 @@
         "right",
     )
     squared = exchange(squared, COLS)
-    new_momentum = by_rows(
-        momentum_kernel, (in_hbm(momentum), in_hbm(gradient), orth, in_hbm(high)), f32(*momentum.shape), name="momentum"
+    new_momentum, high, low = by_rows(
+        momentum_kernel,
+        (in_hbm(momentum), in_hbm(gradient), orth, in_hbm(high), in_hbm(low)),
+        (f32(*momentum.shape), half_width, half_width),
+        name="momentum",
+        steps=2,
     )
     squared, new_momentum = lax.optimization_barrier((squared, new_momentum))
     update, new_factor = by_rows(
         update_kernel,
-        (place, squared, right, orth, in_hbm(high), in_hbm(low)),
+        (place, squared, right, orth, high, low),
         (wide, f32(*right_factor.shape)),
         name="update",
         steps=2,

time: 541 us -> 541 us (level)
  no operation moved by 1% of the time
where the time goes in v3:
time: 541 us; the launch traced here: 530 us
  Pallas kernels  384 us (71%)
  waiting for transfers between devices  46.6 us (9%)
  starting transfers between devices  45.6 us (8%)
  blocking collectives  43.8 us (8%)
  local copies, waits for them, and re-layouts  9.01 us (2%)
    pallas_call x10, Pallas kernels, call(): pl.pallas_call(kernel, out_shape=out, in_specs=[SMEM if a.dtype == jnp.in...  373 us
    all_to_all x2, blocking collectives, exchange(): return lax.all_to_all(a, axes, split_axis=0, concat_axis=0, tiled=True)  43.8 us
    ppermute x37, waiting for transfers between devices, shift(): return lax.ppermute(a, axis, [(i, (i + k) % n) for i in range(n)])  42.7 us
    ppermute x37, starting transfers between devices, shift(): return lax.ppermute(a, axis, [(i, (i + k) % n) for i in range(n)])  41.7 us
  transfers between devices with their start and end apart: 38, of which 25 were waited for; matrix products, arithmetic and copies ran while one was open for 0% of the time, Pallas kernels for 69%

profile of v3, /device:TPU:0, one launch (start us, length us, event | category | flops | bytes accessed | tf_op | source)
XLA Modules:
  0.0 530.3 jit_solution(14086465916229581728)
XLA Ops:
  0.7 2.5 collective-permute-start.1
  3.2 1.4 collective-permute-start.2
  4.6 2.0 copy-done.2
  6.7 1.5 copy-done.4
  9.0 1.2 copy-done
  10.2 3.4 collective-permute-done.1.refs_2_
  16.2 5.5 %left.1 = (f32[128,512]{1,0:T(8,128)S(1)}, f32[128,512]{1,0:T(8,128)S(1)}, f32[128,512]{1,0:T(8,128)S(1)}, f32[128,512]{1,0:T(8,128)S(1)}, f32[128,512]{1,0:T(8,...) custom-call(s32[8]{0:T(128)S(1)} %stack.83.order_ref, s32[1]{0:T(128)} %bitcast.10.y_ref, ...), custom_call_target="tpu_custom_call" | custom-call | flops 1 | bytes 1 | tf_op jit(solution)/shard_map/left/pallas_call | solution.py:319
  21.7 1.7 collective-permute-start.7
  23.4 1.7 collective-permute-start.11
  25.1 1.8 collective-permute-start.9
  27.1 5.1 collective-permute-done.7
  32.7 3.1 collective-permute-start.12
  35.8 2.4 collective-permute-done.9.refs_2_
  38.2 4.5 collective-permute-done.8.refs_1_
  42.8 25.3 %all_to_all.27 = f32[8,32,512]{2,1,0:T(8,128)S(1)} all-to-all(f32[8,32,512]{2,1,0:T(8,128)S(1)} %bitcast.29), channel_id=1, replica_groups=mesh['x'=4,'c'=2,'y'=4,'z'=8] {'z'}, dimensions={0} | all-to-all | bytes 1048576 | tf_op jit(solution)/shard_map/all_to_all | solution.py:44
  68.2 18.5 %all_to_all.28 = f32[8,32,512]{2,1,0:T(8,128)S(1)} all-to-all(f32[8,32,512]{2,1,0:T(8,128)S(1)} %bitcast.28), channel_id=1, replica_groups=mesh['x'=4,'c'=2,'y'=4,'z'=8] {'z'}, dimensions={0} | all-to-all | bytes 1048576 | tf_op jit(solution)/shard_map/all_to_all | solution.py:44
  86.8 2.7 collective-permute-start.13
  89.8 2.9 collective-permute-start.18
  92.7 3.5 collective-permute-done.13.refs_2_.refs_5_
  96.2 3.7 collective-permute-start.14
  100.0 1.9 absorb_own.1
  101.9 1.5 collective-permute-done.17.refs_0_.refs_1_
  103.5 3.1 absorb_near.1
  106.6 0.9 collective-permute-done.16.refs_1_.refs_4_
  107.5 2.5 absorb_far.1
  110.1 3.1 collective-permute-done.19
  113.3 1.4 collective-permute-start.20
  114.7 2.4 collective-permute-start.21
  117.1 1.8 collective-permute-start.22
  118.9 5.4 %collective-permute-done.20.refs_1_ = f32[608,128]{1,0:T(8,128)S(1)} collective-permute-done((f32[608,128]{1,0:T(8,128)S(1)}, f32[608,128]{1,0:T(8,128)S(1)}, u32[]{:S(2)}, u32[]{:S(2)}) %collective-permute-start.20) | collective-permute-done | bytes 311328 | tf_op jit(solution)/shard_map/ppermute | solution.py:31
  124.3 6.9 %collective-permute-done.21.refs_2_ = f32[608,128]{1,0:T(8,128)S(1)} collective-permute-done((f32[608,128]{1,0:T(8,128)S(1)}, f32[608,128]{1,0:T(8,128)S(1)}, u32[]{:S(2)}, u32[]{:S(2)}) %collective-permute-start.21) | collective-permute-done | bytes 311328 | tf_op jit(solution)/shard_map/ppermute | solution.py:31
  131.4 2.0 collective-permute-start.24
  133.4 2.2 collective-permute-start.25
  135.6 1.2 collective-permute-start.26
  137.6 2.4 collective-permute-start.28
  140.9 1.5 collective-permute-start.27
  145.1 352.0 %inverse_factor.1.inverse_ref.refs_8_ = f32[512,512]{1,0:T(8,128)S(1)} custom-call(s32[8]{0:T(128)S(1)} %stack.71.order_ref, f32[160,128]{1,0:T(8,128)S(1)} %get-tuple-element.73.refs_0_, f32[160,128]{1,0:T(8,128)S(1)} %collective-permute-done.24.refs_1_, f32[160,128]{1,0:T(8,128)S(1)} %collective-permute-done.25.refs_2_, ...), custom_call_target="tpu_custom_call" | custom-call | flops 1 | bytes 1 | tf_op jit(solution)/shard_map/inverse_factor/pallas_call | solution.py:319
  497.1 3.9 orth.1.orth_ref
  502.8 0.9 collective-permute-done.34.refs_5_
  504.3 3.9 right.1
  508.2 0.9 copy-done.11
  509.2 1.0 copy-done.12
  510.1 3.8 all-to-all-start.2
  514.0 5.1 momentum.1
  519.1 0.9 copy-done.13
  520.0 3.9 all-to-all-done.2.squared_ref
  524.0 1.2 copy-done.14
  525.2 4.7 update.1
  (84 shorter events, 12.0 us)
Async XLA Ops:
  0.6 9.6 %collective-permute-start = (f32[64,896]{1,0:T(8,128)}, f32[64,896]{1,0:T(8,128)S(1)}, u32[]{:S(2)}, u32[]{:S(2)}) collective-permute-start(f32[64,896]{1,0:T(8,128)} %refs_0_), channel_id=1, source_target_pairs={{0,64},{64,128},{128,192},{192,0},{1,65},{65,129},{129,193},{193,1... | collective-permute-start | bytes 688136 | tf_op jit(solution)/shard_map/ppermute | solution.py:31
  0.7 12.9 %collective-permute-start.1 = (f32[64,896]{1,0:T(8,128)}, f32[64,896]{1,0:T(8,128)S(1)}, u32[]{:S(2)}, u32[]{:S(2)}) collective-permute-start(f32[64,896]{1,0:T(8,128)} %refs_0_), channel_id=1, source_target_pairs={{0,128},{64,192},{128,0},{192,64},{1,129},{65,193},{129,1},{193,65... | collective-permute-start | bytes 688136 | tf_op jit(solution)/shard_map/ppermute | solution.py:31
  3.2 10.4 %collective-permute-start.2 = (f32[64,896]{1,0:T(8,128)}, f32[64,896]{1,0:T(8,128)S(1)}, u32[]{:S(2)}, u32[]{:S(2)}) collective-permute-start(f32[64,896]{1,0:T(8,128)} %refs_0_), channel_id=1, source_target_pairs={{0,192},{64,0},{128,64},{192,128},{1,193},{65,1},{129,65},{193,129... | collective-permute-start | bytes 688136 | tf_op jit(solution)/shard_map/ppermute | solution.py:31
  8.2 5.5 %copy-start.15 = (f32[64,896]{1,0:T(8,128)S(1)}, f32[64,896]{1,0:T(8,128)}, u32[]{:S(2)}) copy-start(f32[64,896]{1,0:T(8,128)} %refs_0_) | copy-start | bytes 688132
  13.6 1.5 collective-permute-start.3
  13.7 1.8 collective-permute-start.4
  14.2 2.0 collective-permute-start.5
  14.2 2.0 collective-permute-start.6
  21.7 10.4 %collective-permute-start.7 = (f32[128,512]{1,0:T(8,128)S(1)}, f32[128,512]{1,0:T(8,128)S(1)}, u32[]{:S(2)}, u32[]{:S(2)}) collective-permute-start(f32[128,512]{1,0:T(8,128)S(1)} %get-tuple-element.58), channel_id=1, source_target_pairs={{0,8},{8,16},{16,24},{24,0},{1,9},{9,17},{17,25},{25,1},{2,10},{10... | collective-permute-start | bytes 786440 | tf_op jit(solution)/shard_map/ppermute | solution.py:31
  23.4 9.3 %collective-permute-start.11 = (f32[128,512]{1,0:T(8,128)S(1)}, f32[128,512]{1,0:T(8,128)S(1)}, u32[]{:S(2)}, u32[]{:S(2)}) collective-permute-start(f32[128,512]{1,0:T(8,128)S(1)} %get-tuple-element.63), channel_id=1, source_target_pairs={{0,24},{8,0},{16,8},{24,16},{1,25},{9,1},{17,9},{25,17},{2,26},{10... | collective-permute-start | bytes 786440 | tf_op jit(solution)/shard_map/ppermute | solution.py:31
  25.1 13.1 %collective-permute-start.9 = (f32[128,512]{1,0:T(8,128)S(1)}, f32[128,512]{1,0:T(8,128)S(1)}, u32[]{:S(2)}, u32[]{:S(2)}) collective-permute-start(f32[128,512]{1,0:T(8,128)S(1)} %get-tuple-element.59), channel_id=1, source_target_pairs={{0,24},{8,0},{16,8},{24,16},{1,25},{9,1},{17,9},{25,17},{2,26},{10... | collective-permute-start | bytes 786440 | tf_op jit(solution)/shard_map/ppermute | solution.py:31
  26.9 11.3 %collective-permute-start.10 = (f32[128,512]{1,0:T(8,128)S(1)}, f32[128,512]{1,0:T(8,128)S(1)}, u32[]{:S(2)}, u32[]{:S(2)}) collective-permute-start(f32[128,512]{1,0:T(8,128)S(1)} %get-tuple-element.61), channel_id=1, source_target_pairs={{0,8},{8,16},{16,24},{24,0},{1,9},{9,17},{17,25},{25,1},{2,10},{10... | collective-permute-start | bytes 786440 | tf_op jit(solution)/shard_map/ppermute | solution.py:31
  32.2 10.5 %collective-permute-start.8 = (f32[128,512]{1,0:T(8,128)S(1)}, f32[128,512]{1,0:T(8,128)S(1)}, u32[]{:S(2)}, u32[]{:S(2)}) collective-permute-start(f32[128,512]{1,0:T(8,128)S(1)} %add.160), channel_id=1, source_target_pairs={{0,8},{8,16},{16,24},{24,0},{1,9},{9,17},{17,25},{25,1},{2,10},{10... | collective-permute-start | bytes 786440 | tf_op jit(solution)/shard_map/ppermute | solution.py:31
  32.7 10.0 %collective-permute-start.12 = (f32[128,512]{1,0:T(8,128)S(1)}, f32[128,512]{1,0:T(8,128)S(1)}, u32[]{:S(2)}, u32[]{:S(2)}) collective-permute-start(f32[128,512]{1,0:T(8,128)S(1)} %add.161), channel_id=1, source_target_pairs={{0,24},{8,0},{16,8},{24,16},{1,25},{9,1},{17,9},{25,17},{2,26},{10... | collective-permute-start | bytes 786440 | tf_op jit(solution)/shard_map/ppermute | solution.py:31
  68.2 31.8 %copy-start.1 = (bf16[1024,896]{1,0:T(8,128)(2,1)S(1)}, bf16[1024,896]{1,0:T(8,128)(2,1)}, u32[]{:S(2)}) copy-start(bf16[1024,896]{1,0:T(8,128)(2,1)} %copy-done) | copy-start | bytes 5505028
  86.7 15.2 %copy-start.3 = (f32[8,32,512]{2,1,0:T(8,128)}, f32[8,32,512]{2,1,0:T(8,128)S(1)}, u32[]{:S(2)}) copy-start(f32[8,32,512]{2,1,0:T(8,128)S(1)} %all_to_all.28) | copy-start | bytes 1572868
  86.8 9.5 %collective-permute-start.13 = (f32[128,512]{1,0:T(8,128)S(1)}, f32[128,512]{1,0:T(8,128)S(1)}, u32[]{:S(2)}, u32[]{:S(2)}) collective-permute-start(f32[128,512]{1,0:T(8,128)S(1)} %bitcast.32), channel_id=1, source_target_pairs={{0,24},{8,0},{16,8},{24,16},{1,25},{9,1},{17,9},{25,17},{2,26},{10... | collective-permute-start | bytes 786440 | tf_op jit(solution)/shard_map/ppermute | solution.py:31
  89.5 10.5 %collective-permute-start.15 = (f32[128,512]{1,0:T(8,128)S(1)}, f32[128,512]{1,0:T(8,128)S(1)}, u32[]{:S(2)}, u32[]{:S(2)}) collective-permute-start(f32[128,512]{1,0:T(8,128)S(1)} %bitcast.30), channel_id=1, source_target_pairs={{0,8},{8,16},{16,24},{24,0},{1,9},{9,17},{17,25},{25,1},{2,10},{10... | collective-permute-start | bytes 786440 | tf_op jit(solution)/shard_map/ppermute | solution.py:31
  89.5 14.0 %collective-permute-start.17 = (f32[128,512]{1,0:T(8,128)S(1)}, f32[128,512]{1,0:T(8,128)S(1)}, u32[]{:S(2)}, u32[]{:S(2)}) collective-permute-start(f32[128,512]{1,0:T(8,128)S(1)} %bitcast.33), channel_id=1, source_target_pairs={{0,8},{8,16},{16,24},{24,0},{1,9},{9,17},{17,25},{25,1},{2,10},{10... | collective-permute-start | bytes 786440 | tf_op jit(solution)/shard_map/ppermute | solution.py:31
  89.8 13.6 %collective-permute-start.18 = (f32[128,512]{1,0:T(8,128)S(1)}, f32[128,512]{1,0:T(8,128)S(1)}, u32[]{:S(2)}, u32[]{:S(2)}) collective-permute-start(f32[128,512]{1,0:T(8,128)S(1)} %bitcast.31), channel_id=1, source_target_pairs={{0,24},{8,0},{16,8},{24,16},{1,25},{9,1},{17,9},{25,17},{2,26},{10... | collective-permute-start | bytes 786440 | tf_op jit(solution)/shard_map/ppermute | solution.py:31
  96.2 7.2 %copy-start.5 = (f32[128,512]{1,0:T(8,128)}, f32[128,512]{1,0:T(8,128)S(1)}, u32[]{:S(2)}) copy-start(f32[128,512]{1,0:T(8,128)S(1)} %collective-permute-done.13.refs_2_.refs_5_) | copy-start | bytes 786436
  96.2 10.4 %collective-permute-start.14 = (f32[128,512]{1,0:T(8,128)S(1)}, f32[128,512]{1,0:T(8,128)S(1)}, u32[]{:S(2)}, u32[]{:S(2)}) collective-permute-start(f32[128,512]{1,0:T(8,128)S(1)} %collective-permute-done.13.refs_2_.refs_5_), channel_id=1, source_target_pairs={{0,24},{8,0},{16,8},{24,16},{1,25},{9,1},{17,9},{25,17},{2,26},{10... | collective-permute-start | bytes 786440 | tf_op jit(solution)/shard_map/ppermute | solution.py:31
  99.9 3.5 copy-start.6
  99.9 7.6 %collective-permute-start.16 = (f32[128,512]{1,0:T(8,128)S(1)}, f32[128,512]{1,0:T(8,128)S(1)}, u32[]{:S(2)}, u32[]{:S(2)}) collective-permute-start(f32[128,512]{1,0:T(8,128)S(1)} %collective-permute-done.15.refs_1_.refs_2_), channel_id=1, source_target_pairs={{0,8},{8,16},{16,24},{24,0},{1,9},{9,17},{17,25},{25,1},{2,10},{10... | collective-permute-start | bytes 786440 | tf_op jit(solution)/shard_map/ppermute | solution.py:31
  103.4 3.1 copy-start.7
  103.4 3.1 copy-start.8
  106.6 3.5 copy-start.9
  107.5 2.5 copy-start.10
  110.1 3.2 collective-permute-start.19
  113.3 11.0 %collective-permute-start.20 = (f32[608,128]{1,0:T(8,128)S(1)}, f32[608,128]{1,0:T(8,128)S(1)}, u32[]{:S(2)}, u32[]{:S(2)}) collective-permute-start(f32[608,128]{1,0:T(8,128)S(1)} %get-tuple-element.95), channel_id=1, source_target_pairs={{0,64},{64,128},{128,192},{192,0},{1,65},{65,129},{129,193},{193,1... | collective-permute-start | bytes 933896 | tf_op jit(solution)/shard_map/ppermute | solution.py:31
  114.7 16.4 %collective-permute-start.21 = (f32[608,128]{1,0:T(8,128)S(1)}, f32[608,128]{1,0:T(8,128)S(1)}, u32[]{:S(2)}, u32[]{:S(2)}) collective-permute-start(f32[608,128]{1,0:T(8,128)S(1)} %get-tuple-element.94), channel_id=1, source_target_pairs={{0,128},{64,192},{128,0},{192,64},{1,129},{65,193},{129,1},{193,65... | collective-permute-start | bytes 933896 | tf_op jit(solution)/shard_map/ppermute | solution.py:31
  117.1 14.2 %collective-permute-start.22 = (f32[608,128]{1,0:T(8,128)S(1)}, f32[608,128]{1,0:T(8,128)S(1)}, u32[]{:S(2)}, u32[]{:S(2)}) collective-permute-start(f32[608,128]{1,0:T(8,128)S(1)} %get-tuple-element.93), channel_id=1, source_target_pairs={{0,192},{64,0},{128,64},{192,128},{1,193},{65,1},{129,65},{193,129... | collective-permute-start | bytes 933896 | tf_op jit(solution)/shard_map/ppermute | solution.py:31
  131.4 369.7 %copy-start.16 = (f32[448,128]{1,0:T(8,128)}, f32[448,128]{1,0:T(8,128)S(1)}, u32[]{:S(2)}) copy-start(f32[448,128]{1,0:T(8,128)S(1)} %get-tuple-element.77.refs_0_) | copy-start | bytes 688132
  131.4 8.6 %collective-permute-start.24 = (f32[160,128]{1,0:T(8,128)S(1)}, f32[160,128]{1,0:T(8,128)S(1)}, u32[]{:S(2)}, u32[]{:S(2)}) collective-permute-start(f32[160,128]{1,0:T(8,128)S(1)} %get-tuple-element.73.refs_0_), channel_id=1, source_target_pairs={{0,64},{64,128},{128,192},{192,0},{1,65},{65,129},{129,193},{193,1... | collective-permute-start | bytes 245768 | tf_op jit(solution)/shard_map/ppermute | solution.py:31
  133.4 7.2 %collective-permute-start.25 = (f32[160,128]{1,0:T(8,128)S(1)}, f32[160,128]{1,0:T(8,128)S(1)}, u32[]{:S(2)}, u32[]{:S(2)}) collective-permute-start(f32[160,128]{1,0:T(8,128)S(1)} %get-tuple-element.73.refs_0_), channel_id=1, source_target_pairs={{0,128},{64,192},{128,0},{192,64},{1,129},{65,193},{129,1},{193,65... | collective-permute-start | bytes 245768 | tf_op jit(solution)/shard_map/ppermute | solution.py:31
  135.6 5.3 %collective-permute-start.26 = (f32[160,128]{1,0:T(8,128)S(1)}, f32[160,128]{1,0:T(8,128)S(1)}, u32[]{:S(2)}, u32[]{:S(2)}) collective-permute-start(f32[160,128]{1,0:T(8,128)S(1)} %get-tuple-element.73.refs_0_), channel_id=1, source_target_pairs={{0,192},{64,0},{128,64},{192,128},{1,193},{65,1},{129,65},{193,129... | collective-permute-start | bytes 245768 | tf_op jit(solution)/shard_map/ppermute | solution.py:31
  136.8 364.2 %collective-permute-start.23 = (f32[448,128]{1,0:T(8,128)S(1)}, f32[448,128]{1,0:T(8,128)}, u32[]{:S(2)}, u32[]{:S(2)}) collective-permute-start(f32[448,128]{1,0:T(8,128)S(1)} %get-tuple-element.77.refs_0_), channel_id=1, source_target_pairs={{0,64},{64,128},{128,192},{192,0},{1,65},{65,129},{129,193},{193,1... | collective-permute-start | bytes 688136 | tf_op jit(solution)/shard_map/ppermute | solution.py:31
  137.6 363.4 %collective-permute-start.28 = (f32[448,128]{1,0:T(8,128)S(1)}, f32[448,128]{1,0:T(8,128)}, u32[]{:S(2)}, u32[]{:S(2)}) collective-permute-start(f32[448,128]{1,0:T(8,128)S(1)} %get-tuple-element.77.refs_0_), channel_id=1, source_target_pairs={{0,192},{64,0},{128,64},{192,128},{1,193},{65,1},{129,65},{193,129... | collective-permute-start | bytes 688136 | tf_op jit(solution)/shard_map/ppermute | solution.py:31
  140.9 360.2 %collective-permute-start.27 = (f32[448,128]{1,0:T(8,128)S(1)}, f32[448,128]{1,0:T(8,128)}, u32[]{:S(2)}, u32[]{:S(2)}) collective-permute-start(f32[448,128]{1,0:T(8,128)S(1)} %get-tuple-element.77.refs_0_), channel_id=1, source_target_pairs={{0,128},{64,192},{128,0},{192,64},{1,129},{65,193},{129,1},{193,65... | collective-permute-start | bytes 688136 | tf_op jit(solution)/shard_map/ppermute | solution.py:31
  142.4 1.3 collective-permute-start.29
  142.4 1.4 collective-permute-start.30
  143.7 1.3 collective-permute-start.31
  143.8 1.3 collective-permute-start.32
  501.0 1.7 collective-permute-start.33
  501.5 2.1 collective-permute-start.34
  502.0 2.0 collective-permute-start.35
  502.3 2.0 collective-permute-start.36
  510.1 13.9 %all-to-all-start.2 = ((f32[32,4,128]{2,1,0:T(4,128)}), f32[32,4,128]{2,1,0:T(4,128)S(1)}, u32[]{:S(2)}, u32[]{:S(2)}) async-start(f32[32,4,128]{2,1,0:T(4,128)} %get-tuple-element.81), calls=%async_computation.2 | async-start | bytes 131072 | tf_op jit(solution)/shard_map/all_to_all | solution.py:44
  (7 other events, 8.8 us)
